TPU v7x, 256 devices: a whole 4x4x8 slice. The times are simulated.
256 devices in a mesh: group: 8 (over x, core), brick: 32 (over y, z).
Axes of the slice: x: 4, y: 4, z: 8, core: 2. Of those that a mesh axis runs over, the one named last changes fastest.
Arguments:
- noise_level0: float32 [8, 64, 16], P('group', 'brick'), may hold values from -6 to 6
- noise_level1: float32 [16, 128, 32], P('group', 'brick'), may hold values from -6 to 6
- noise_level2: float32 [32, 256, 64], P('group', 'brick'), may hold values from -6 to 6
- noise_level3: float32 [64, 512, 128], P('group', 'brick'), may hold values from -6 to 6
- noise_level4: float32 [128, 1024, 256], P('group', 'brick'), may hold values from -6 to 6
- refine_kernels: float32 [4, 8, 27], replicated, may hold values from -1.25 to 1.25
- noise_kernels: float32 [4, 8, 8], replicated, may hold values from -2 to 2
- cotangent: float32 [128, 1024, 256], P('group', 'brick'), may hold values from -6 to 6
Outputs:
- density: float32 [128, 1024, 256], P('group', 'brick')
- grad_level0: float32 [8, 64, 16], P('group', 'brick')
- grad_level1: float32 [16, 128, 32], P('group', 'brick')
- grad_level2: float32 [32, 256, 64], P('group', 'brick')
- grad_level3: float32 [64, 512, 128], P('group', 'brick')
- grad_level4: float32 [128, 1024, 256], P('group', 'brick')
All inputs are finite; a program needn't handle non-finite values.
Results may differ from a plain program's by a relative error of at most 0.0002.
Values sent between devices are 32-bit elements; how exact they have to be, the bound alone decides.
A program may use at most 128 MiB of HBM per device.

v0:
```python
import jax
import jax.numpy as jnp
from jax import lax
from jax.experimental import pallas as pl
from jax.experimental.pallas import tpu as pltpu
from jax.sharding import PartitionSpec as P

LEVELS = 4
F32 = jnp.float32
BF16 = jnp.bfloat16
MESH = pl.DeviceIdType.MESH

NEAR = [(dx, dy) for dx in (-1, 0, 1) for dy in (-1, 0, 1) if (dx, dy) != (0, 0)]
FAR = [(dx, dy) for dx in (-2, 2) for dy in (-1, 0, 1)]
DIRS = NEAR + FAR


def up8(n):
    return -(-n // 8) * 8


class Plan:
    def __init__(self, shapes):
        self.block = shapes
        self.pairs = {}
        for level in range(1, LEVELS + 1):
            grow = 0 if level == LEVELS else 2
            self.pairs[level] = (shapes[level][0] // 2 + grow, shapes[level][1] // 2 + grow)
        self.rows = {level: up8(2 * ny) for level, (_, ny) in self.pairs.items()}
        self.ext = [
            (shapes[level][0] + 4, up8(shapes[level][1] + 4), 128) for level in range(LEVELS)
        ]
        self.pieces = {}
        self.offset = {}
        total = 0
        for dx, dy in DIRS:
            rows = 0
            pieces = []
            for level in range(LEVELS):
                if abs(dx) == 2 and level > 0:
                    continue
                bx, by = shapes[level][0], shapes[level][1]
                count_x = bx if dx == 0 else min(2, bx)
                count_y = by if dy == 0 else 2
                pieces.append((level, rows, count_x, count_y))
                rows += count_x * count_y
            self.pieces[dx, dy] = pieces
            self.offset[dx, dy] = (total, up8(rows))
            total += up8(rows)
        self.message_rows = total


def inner(step, size):
    if step == 0 or size == 1:
        return 2
    return 2 if step < 0 else size


def outer(step, size):
    if step == 0:
        return 2
    if size == 1:
        return 2 + step
    return 0 if step < 0 else size + 2


def lane_iota(shape):
    return lax.broadcasted_iota(jnp.int32, shape, len(shape) - 1)


def row_iota(shape):
    return lax.broadcasted_iota(jnp.int32, shape, len(shape) - 2)


def split(values):
    high = values.astype(BF16)
    return high, (values - high.astype(F32)).astype(BF16)


def select_dot(values, matrix):
    high, low = split(values)
    return jnp.dot(high, matrix, preferred_element_type=F32) + jnp.dot(
        low, matrix, preferred_element_type=F32
    )


def merge_matrix(size, width):
    row, col = row_iota((256, width)), lane_iota((256, width))
    parity = (row >= 128).astype(jnp.int32)
    at = row - 128 * parity
    return jnp.where((col == 2 * at + parity) & (at < size), 1.0, 0.0).astype(BF16)


def part_matrix(size, width):
    row, col = row_iota((width, 256)), lane_iota((width, 256))
    parity = (col >= 128).astype(jnp.int32)
    at = col - 128 * parity
    return jnp.where((row == 2 * at + parity) & (at < size), 1.0, 0.0).astype(BF16)


def parities():
    shape = (8, 128)
    return row_iota(shape) % 2 == 0, lane_iota(shape) % 2 == 0


def noise_patterns(read, store, transpose):
    even_row, even_lane = parities()
    for p in range(2):
        for other in range(2):
            for dq in range(2):
                for dr in range(2):
                    value = {}
                    for q in range(2):
                        for r in range(2):
                            here = 4 * p + 2 * q + r
                            there = 4 * other + 2 * (q ^ dq) + (r ^ dr)
                            value[q, r] = read(there, here) if transpose else read(here, there)
                    store(
                        p * 8 + other * 4 + dq * 2 + dr,
                        jnp.where(
                            even_row,
                            jnp.where(even_lane, value[0, 0], value[0, 1]),
                            jnp.where(even_lane, value[1, 0], value[1, 1]),
                        ),
                    )


def swaps(tile):
    even_row, even_lane = parities()

    def lanes(v):
        return jnp.where(even_lane, pltpu.roll(v, 127, 1), pltpu.roll(v, 1, 1))

    turned = jnp.where(even_row, pltpu.roll(tile, 7, 0), pltpu.roll(tile, 1, 0))
    return [tile, lanes(tile), turned, lanes(turned)]


def mix(first, second, weights):
    terms = swaps(first) + swaps(second)
    results = []
    for p in range(2):
        total = weights[p * 8] * terms[0]
        for at in range(1, 8):
            total = total + weights[p * 8 + at] * terms[at]
        results.append(total)
    return results


def shift_down(values, size):
    lane = lane_iota(values.shape)
    return jnp.where((lane > 0) & (lane < size), pltpu.roll(values, 1, 1), 0.0)


def shift_up(values, size):
    lane = lane_iota(values.shape)
    return jnp.where(lane < size - 1, pltpu.roll(values, 127, 1), 0.0)


def main_kernel(
    plan,
    noise0, noise1, noise2, noise3, refine_k, noise_k, cotangent,
    fine_out, grad0, grad1, grad2, grad3,
    ext0, ext1, ext2, ext3, part0, part1, part2, part3,
    field1, field2, field3, grads1, grads2, grads3,
    pattern, mixing, mixing_t, cot, shifted, spread, sums, split_g, taps, pooled,
    send_a, recv_a, send_b, recv_b,
    cot_sem, send_a_sem, recv_a_sem, send_b_sem, recv_b_sem,
):
    group, brick = lax.axis_index("group"), lax.axis_index("brick")
    groups, bricks = lax.axis_size("group"), lax.axis_size("brick")
    ext = [ext0, ext1, ext2, ext3]
    part = [part0, part1, part2, part3]
    field = [ext0, field1, field2, field3]
    grads = [part0, grads1, grads2, grads3]

    def neighbour(dx, dy):
        return (
            lax.rem(group + (dx + groups), groups),
            lax.rem(brick + (dy + bricks), bricks),
        )

    barrier = pltpu.get_barrier_semaphore()
    for dx, dy in DIRS:
        pl.semaphore_signal(barrier, inc=1, device_id=neighbour(dx, dy), device_id_type=MESH)

    cot_chunks = cot_sem.shape[0]
    chunk = cot.shape[0] // cot_chunks
    cot_copies = []
    for at in range(cot_chunks):
        copy = pltpu.make_async_copy(
            cotangent.at[pl.ds(at * chunk, chunk)], cot.at[pl.ds(at * chunk, chunk)], cot_sem.at[at]
        )
        copy.start()
        cot_copies.append(copy)

    for level, source in enumerate((noise0, noise1, noise2, noise3)):
        bx, by, size = plan.block[level]
        ext[level][...] = jnp.zeros(ext[level].shape, F32)
        if level:
            grads[level][...] = jnp.zeros(grads[level].shape, F32)
        part[level][...] = jnp.zeros(part[level].shape, F32)
        ext[level][2 : 2 + bx, 2 : 2 + by, 0:size] = source[...]

    def pack(source, target, start_of, sign):
        for dx, dy in DIRS:
            base, _ = plan.offset[dx, dy]
            for level, row, count_x, count_y in plan.pieces[dx, dy]:
                bx, by, _ = plan.block[level]
                x0, y0 = start_of(sign * dx, bx), start_of(sign * dy, by)
                for i in range(count_x):
                    target[pl.ds(base + row + i * count_y, count_y), :] = source[level][
                        x0 + i, y0 : y0 + count_y, :
                    ]

    def unpack(source, target, start_of, add):
        for dx, dy in DIRS:
            base, _ = plan.offset[dx, dy]
            for level, row, count_x, count_y in plan.pieces[dx, dy]:
                bx, by, _ = plan.block[level]
                x0, y0 = start_of(-dx, bx), start_of(-dy, by)
                for i in range(count_x):
                    value = source[pl.ds(base + row + i * count_y, count_y), :]
                    if add:
                        value = value + target[level][x0 + i, y0 : y0 + count_y, :]
                    target[level][x0 + i, y0 : y0 + count_y, :] = value

    def copies(source, target, send_sem, recv_sem):
        made = []
        for at, (dx, dy) in enumerate(DIRS):
            base, rows = plan.offset[dx, dy]
            made.append(
                pltpu.make_async_remote_copy(
                    src_ref=source.at[pl.ds(base, rows)],
                    dst_ref=target.at[pl.ds(base, rows)],
                    send_sem=send_sem.at[at],
                    recv_sem=recv_sem.at[at],
                    device_id=neighbour(dx, dy),
                    device_id_type=MESH,
                )
            )
        return made

    send_a[...] = jnp.zeros(send_a.shape, F32)
    send_b[...] = jnp.zeros(send_b.shape, F32)
    pack(ext, send_a, inner, 1)
    pl.semaphore_wait(barrier, len(DIRS))
    out_a = copies(send_a, recv_a, send_a_sem, recv_a_sem)
    for copy in out_a:
        copy.start()

    even_row, _ = parities()

    def build(level, carry):
        for o in range(27):
            for p in range(2):
                for r in range(2):
                    pattern[level, o * 4 + p * 2 + r] = jnp.where(
                        even_row,
                        refine_k[level, 4 * p + r, o],
                        refine_k[level, 4 * p + 2 + r, o],
                    )
        return carry

    lax.fori_loop(0, LEVELS, build, 0)

    def build_mixing(level, carry):
        def read(u, v):
            return noise_k[level, u, v]

        def store(at, value):
            mixing[level, at] = value

        def store_t(at, value):
            mixing_t[level, at] = value

        noise_patterns(read, store, False)
        noise_patterns(read, store_t, True)
        return carry

    lax.fori_loop(0, LEVELS - 1, build_mixing, 0)

    def inside(level, x_at, shape, first_row, first_x):
        bx, by, _ = plan.block[level]
        y = row_iota(shape) + (brick * by - 2 + first_row)
        x = group * bx - 2 + first_x + x_at
        limit = jnp.where((x >= 0) & (x < groups * bx), bricks * by, 0)
        return (y >= 0) & (y < limit)

    def tile_rows(at):
        return pl.ds(8 * at, 8)

    def adjoint(level):
        nx, ny = plan.pairs[level]
        rows = plan.rows[level]
        size = plan.block[level][2] // 2
        tiles = rows // 8
        if level == LEVELS:
            matrix = part_matrix(size, 256)
            for at in range(cot_chunks):
                cot_copies[at].wait()

            def part_chunk(at, carry):
                rows_in = cot[pl.ds(at * chunk, chunk)].reshape(chunk * rows, 256)
                both = select_dot(rows_in, matrix)
                for r in range(2):
                    split_g[r, pl.ds(at * chunk, chunk), 0:rows, :] = both[
                        :, 128 * r : 128 * (r + 1)
                    ].reshape(chunk, rows, 128)
                return carry

            lax.fori_loop(0, cot_chunks, part_chunk, 0)
        else:
            both = select_dot(
                grads[level][:, 0:rows, :].reshape(2 * nx * rows, 128), part_matrix(size, 128)
            )
            for r in range(2):
                split_g[r, 0 : 2 * nx, 0:rows, :] = both[:, 128 * r : 128 * (r + 1)].reshape(
                    2 * nx, rows, 128
                )

        for tap in range(9):
            for edge in (0, nx + 1):
                taps[tap, edge, 0:rows, :] = jnp.zeros((rows, 128), F32)

        for s in (1, 0, 2):
            weights = [pattern[level - 1, s * 36 + at] for at in range(36)]

            def step(i, carry):
                for tile in range(tiles):
                    here = tile_rows(tile)
                    values = [split_g[r, 2 * i + p, here, :] for p in range(2) for r in range(2)]
                    for tap in range(9):
                        total = weights[tap * 4] * values[0]
                        for at in range(1, 4):
                            total = total + weights[tap * 4 + at] * values[at]
                        if s != 1:
                            total = total + taps[tap, i + s, here, :]
                        taps[tap, i + s, here, :] = total
                return carry

            lax.fori_loop(0, nx, step, 0)

        target = grads[level - 1]
        first = 1 if level == LEVELS else 0

        def combine(x, carry):
            for t in range(3):
                pooled[t, 0:8, :] = jnp.zeros((8, 128), F32)
                pooled[t, pl.ds(8 + rows, 8), :] = jnp.zeros((8, 128), F32)
                for tile in range(tiles):
                    here = tile_rows(tile)
                    pooled[t, pl.ds(8 + 8 * tile, 8), :] = (
                        taps[3 * t + 1, x, here, :]
                        + shift_up(taps[3 * t, x, here, :], size)
                        + shift_down(taps[3 * t + 2, x, here, :], size)
                    )
            total = None
            for t in range(3):
                for q in range(2):
                    value = pooled[t, pl.ds(8 - 2 * t + q, ny + 2, stride=2), :]
                    total = value if total is None else total + value
            keep = inside(level - 1, x, (ny + 2, 128), first, first)
            target[x + first, first : first + ny + 2, :] = jnp.where(keep, total, 0.0)
            return carry

        lax.fori_loop(0, nx + 2, combine, 0)

    def mix_level(level, source, target, weights_of, masked):
        nx, _ = plan.pairs[level]
        weights = [weights_of[level - 1, at] for at in range(16)]

        def step(i, carry):
            for tile in range(plan.rows[level] // 8):
                here = tile_rows(tile)
                mixed = mix(source[2 * i, here, :], source[2 * i + 1, here, :], weights)
                for p in range(2):
                    value = mixed[p]
                    if masked:
                        value = value + target[2 * i + p, here, :]
                        keep = inside(level, 2 * i + p, (8, 128), 8 * tile, 0)
                        value = jnp.where(keep, value, 0.0)
                    target[2 * i + p, here, :] = value
            return carry

        lax.fori_loop(0, nx, step, 0)

    for level in range(LEVELS, 0, -1):
        adjoint(level)
        if level > 1:
            mix_level(level - 1, grads[level - 1], part[level - 1], mixing_t, False)

    pack(part, send_b, outer, 1)
    out_b = copies(send_b, recv_b, send_b_sem, recv_b_sem)
    for copy in out_b:
        copy.start()

    for copy in out_a:
        copy.wait_recv()
    unpack(recv_a, ext, outer, False)
    for x in range(ext0.shape[0]):
        keep = inside(0, x, ext0.shape[1:], 0, 0)
        ext0[x] = jnp.where(keep, ext0[x], 0.0)

    def forward(level):
        nx, ny = plan.pairs[level]
        rows = plan.rows[level]
        size = plan.block[level][2] // 2
        first = 1 if level == LEVELS else 0
        source = field[level - 1]
        count = up8(ny + 2)
        target = fine_out if level == LEVELS else sums

        def widen(x, carry):
            for tile in range(count // 8):
                value = source[x + first, pl.ds(first + 8 * tile, 8), :]
                for w, moved in enumerate((shift_down(value, size), value, shift_up(value, size))):
                    for q in range(2):
                        spread[w, x, pl.ds(16 * tile + q, 8, stride=2), :] = moved
            return carry

        lax.fori_loop(0, nx + 2, widen, 0)

        for s in range(3):
            weights = [pattern[level - 1, s * 36 + at] for at in range(36)]

            def step(i, carry):
                for tile in range(rows // 8):
                    here = tile_rows(tile)
                    totals = [None] * 4
                    for tap in range(9):
                        value = spread[tap % 3, i + s, pl.ds(8 * tile + 2 * (tap // 3), 8), :]
                        for at in range(4):
                            term = weights[tap * 4 + at] * value
                            totals[at] = term if totals[at] is None else totals[at] + term
                    for at in range(4):
                        p, r = at // 2, at % 2
                        value = totals[at]
                        if s:
                            value = value + target[r, 2 * i + p, here, :]
                        target[r, 2 * i + p, here, :] = value
                return carry

            lax.fori_loop(0, nx, step, 0)

        if level < LEVELS:
            both = jnp.concatenate(
                [sums[r, 0 : 2 * nx, 0:rows, :].reshape(2 * nx * rows, 128) for r in range(2)],
                axis=1,
            )
            fine = select_dot(both, merge_matrix(size, 128))
            field[level][:, 0:rows, :] = fine.reshape(2 * nx, rows, 128)
            mix_level(level, ext[level], field[level], mixing, True)

    for level in range(1, LEVELS + 1):
        forward(level)

    for copy in out_b:
        copy.wait_recv()
    unpack(recv_b, part, inner, True)
    for level, target in enumerate((grad0, grad1, grad2, grad3)):
        bx, by, size = plan.block[level]
        target[...] = part[level][2 : 2 + bx, 2 : 2 + by, 0:size]
    for copy in out_a + out_b:
        copy.wait_send()


def finish_kernel(
    fine, noise, cotangent, noise_k, in0, in1, in2, in3,
    density, grad, grad0, grad1, grad2, grad3, mixing, mixing_t,
):
    @pl.when(pl.program_id(0) == 0)
    def _():
        def read(u, v):
            return noise_k[LEVELS - 1, u, v]

        def store(at, value):
            mixing[at] = value

        def store_t(at, value):
            mixing_t[at] = value

        noise_patterns(read, store, False)
        noise_patterns(read, store_t, True)
        for source, target in ((in0, grad0), (in1, grad1), (in2, grad2), (in3, grad3)):
            target[...] = source[...]

    size_x, rows, _ = noise.shape
    both = jnp.concatenate([fine[r].reshape(size_x * rows, 128) for r in range(2)], axis=1)
    density[...] = select_dot(both, merge_matrix(128, 256)).reshape(size_x, rows, 256)
    for source, target, weights_of, add in (
        (noise, density, mixing, True),
        (cotangent, grad, mixing_t, False),
    ):
        weights = [weights_of[at] for at in range(16)]

        def step(i, carry):
            for tile in range(rows // 8):
                for half in range(2):
                    here, lanes = pl.ds(8 * tile, 8), pl.ds(128 * half, 128)
                    mixed = mix(
                        source[2 * i, here, lanes], source[2 * i + 1, here, lanes], weights
                    )
                    for p in range(2):
                        value = mixed[p]
                        if add:
                            value = value + target[2 * i + p, here, lanes]
                        target[2 * i + p, here, lanes] = value
            return carry

        lax.fori_loop(0, size_x // 2, step, 0)


def body(
    noise_level0,
    noise_level1,
    noise_level2,
    noise_level3,
    noise_level4,
    refine_kernels,
    noise_kernels,
    cotangent,
):
    noises = (noise_level0, noise_level1, noise_level2, noise_level3, noise_level4)
    plan = Plan([noise.shape for noise in noises])
    nx, ny = plan.pairs[LEVELS]
    rows = plan.rows[LEVELS]
    vmem = pl.BlockSpec(memory_space=pltpu.VMEM)
    smem = pl.BlockSpec(memory_space=pltpu.SMEM)
    anywhere = pl.BlockSpec(memory_space=pl.ANY)

    def scratch(*shape):
        return pltpu.VMEM(shape, F32)

    def field_shape(level):
        grown = plan.ext[level]
        return (grown[0], grown[1] + 8, 128)

    messages = [scratch(plan.message_rows, 128)] * 4
    count = len(DIRS)
    fine, grad0, grad1, grad2, grad3 = pl.pallas_call(
        lambda *refs: main_kernel(plan, *refs),
        out_shape=[jax.ShapeDtypeStruct((2, 2 * nx, rows, 128), F32)]
        + [jax.ShapeDtypeStruct(noise.shape, F32) for noise in noises[:LEVELS]],
        in_specs=[vmem] * 4 + [smem] * 2 + [anywhere],
        out_specs=[vmem] * 5,
        scratch_shapes=[scratch(*shape) for shape in plan.ext]
        + [scratch(*shape) for shape in plan.ext]
        + [scratch(*field_shape(level)) for level in (1, 2, 3)]
        + [scratch(*plan.ext[level]) for level in (1, 2, 3)]
        + [
            scratch(LEVELS, 108, 8, 128),
            scratch(LEVELS - 1, 16, 8, 128),
            scratch(LEVELS - 1, 16, 8, 128),
            scratch(*cotangent.shape),
            scratch(8, 128),
            scratch(3, nx + 2, 2 * up8(ny + 2), 128),
            scratch(2, 2 * nx, rows, 128),
            scratch(2, 2 * nx, rows, 128),
            scratch(9, nx + 2, rows, 128),
            scratch(3, rows + 16, 128),
        ]
        + messages
        + [pltpu.SemaphoreType.DMA((4,))]
        + [pltpu.SemaphoreType.DMA((count,))] * 4,
        compiler_params=pltpu.CompilerParams(
            collective_id=0, has_side_effects=True, vmem_limit_bytes=32 * 1024 * 1024
        ),
    )(*noises[:LEVELS], refine_kernels, noise_kernels, cotangent)

    steps = 4
    size_x, size_y, size_z = noise_level4.shape
    block = pl.BlockSpec((size_x // steps, size_y, size_z), lambda i: (i, 0, 0))
    whole = [pl.BlockSpec(noise.shape, lambda i: (0, 0, 0)) for noise in noises[:LEVELS]]
    density, grad4, *small = pl.pallas_call(
        finish_kernel,
        grid=(steps,),
        out_shape=[jax.ShapeDtypeStruct(noise_level4.shape, F32)] * 2
        + [jax.ShapeDtypeStruct(noise.shape, F32) for noise in noises[:LEVELS]],
        in_specs=[
            pl.BlockSpec((2, size_x // steps, rows, 128), lambda i: (0, i, 0, 0)),
            block,
            block,
            smem,
        ]
        + whole,
        out_specs=[block, block] + whole,
        scratch_shapes=[scratch(16, 8, 128), scratch(16, 8, 128)],
        compiler_params=pltpu.CompilerParams(vmem_limit_bytes=32 * 1024 * 1024),
    )(fine, noise_level4, cotangent, noise_kernels, grad0, grad1, grad2, grad3)
    return (density, *small[:1], *small[1:], grad4)


def solution(mesh):
    placed = P("group", "brick", None)
    return jax.shard_map(
        body,
        mesh=mesh,
        in_specs=(placed,) * 5 + (P(), P(), placed),
        out_specs=(placed,) * 6,
        check_vma=False,
    )
```

profile of v0, /device:TPU:1, one launch (start us, length us, event | category | flops | bytes accessed | tf_op | source)
XLA Modules:
  0.0 39.5 jit_solution(8464297473372775850)
XLA Ops:
  0.6 0.0 copy-start
  0.6 1.0 %copy-done = f32[16,32,256]{2,1,0:T(8,128)S(1)} copy-done((f32[16,32,256]{2,1,0:T(8,128)S(1)}, f32[16,32,256]{2,1,0:T(8,128)}, u32[]{:S(2)}) %copy-start) | copy-done | bytes 524312
  1.7 0.0 copy-start.3
  1.7 0.7 %copy-done.3 = f32[4,8,8]{2,1,0:T(8,128)S(1)} copy-done((f32[4,8,8]{2,1,0:T(8,128)S(1)}, f32[4,8,8]{2,1,0:T(8,128)}, u32[]{:S(2)}) %copy-start.3) | copy-done | bytes 1048
  2.4 0.0 copy-start.5
  2.4 0.8 %copy-done.5 = f32[8,16,128]{2,1,0:T(8,128)S(1)} copy-done((f32[8,16,128]{2,1,0:T(8,128)S(1)}, f32[8,16,128]{2,1,0:T(8,128)}, u32[]{:S(2)}) %copy-start.5) | copy-done | bytes 65560
  3.2 0.0 copy-start.6
  3.2 0.7 %copy-done.6 = f32[4,8,64]{2,1,0:T(8,128)S(1)} copy-done((f32[4,8,64]{2,1,0:T(8,128)S(1)}, f32[4,8,64]{2,1,0:T(8,128)}, u32[]{:S(2)}) %copy-start.6) | copy-done | bytes 8216
  4.0 0.0 copy-start.7
  4.0 0.7 %copy-done.7 = f32[4,8,27]{2,1,0:T(8,128)S(1)} copy-done((f32[4,8,27]{2,1,0:T(8,128)S(1)}, f32[4,8,27]{2,1,0:T(8,128)}, u32[]{:S(2)}) %copy-start.7) | copy-done | bytes 3480
  4.7 0.0 copy-start.8
  4.7 0.7 %copy-done.8 = f32[2,4,32]{2,1,0:T(4,128)S(1)} copy-done((f32[2,4,32]{2,1,0:T(4,128)S(1)}, f32[2,4,32]{2,1,0:T(4,128)}, u32[]{:S(2)}) %copy-start.8) | copy-done | bytes 1048
  5.4 0.0 copy-start.9
  5.4 0.7 %copy-done.9 = f32[1,2,16]{2,1,0:T(2,128)S(1)} copy-done((f32[1,2,16]{2,1,0:T(2,128)S(1)}, f32[1,2,16]{2,1,0:T(2,128)}, u32[]{:S(2)}) %copy-start.9) | copy-done | bytes 152
  6.0 0.0 copy-start.1
  6.0 0.0 copy-start.4
  6.0 27.7 %shard_map.127 = (f32[2,16,32,128]{3,2,1,0:T(8,128)S(1)}, f32[1,2,16]{2,1,0:T(2,128)S(1)}, f32[2,4,32]{2,1,0:T(4,128)S(1)}, f32[4,8,64]{2,1,0:T(8,128)S(1)}, f32[8,16,128]{2,1,0:T(8,128)S(1)}) custom-call(f32[1,2,16]{2,1,0:T(2,128)S(1)} %copy-done.9, f32[2,4,32]{2,1,0:T(4,128)S(1)} %copy-done.8, f32[4,8,64]{2,1,0:T(8,128)S(1)} %copy-done.6, ...), custom_call_target="tpu_custom_call" | custom-call | tf_op jit(solution)/shard_map/pallas_call | solution.py:540
  33.7 0.0 copy-done.1
  33.7 0.0 copy-done.4
  33.7 0.0 copy-start.2
  33.7 1.0 %copy-done.2 = f32[16,32,256]{2,1,0:T(8,128)S(1)} copy-done((f32[16,32,256]{2,1,0:T(8,128)S(1)}, f32[16,32,256]{2,1,0:T(8,128)}, u32[]{:S(2)}) %copy-start.2) | copy-done | bytes 524312
  34.8 4.8 %shard_map.128 = (f32[16,32,256]{2,1,0:T(8,128)}, f32[16,32,256]{2,1,0:T(8,128)}, f32[1,2,16]{2,1,0:T(2,128)}, f32[2,4,32]{2,1,0:T(4,128)}, f32[4,8,64]{2,1,0:T(8,128)}, /*index=5*/f32[8,16,128]{2,1,0:T(8,128)}) custom-call(f32[2,16,32,128]{3,2,1,0:T(8,128)S(1)} %get-tuple-element.17.fine, f32[16,32,256]{2,1,0:T(8,128)S(1)} %copy-done.2, ...), custom_call_target="tpu_custom_call" | custom-call | tf_op jit(solution)/shard_map/pallas_call | solution.py:574
Async XLA Ops:
  0.6 1.0 %copy-start = (f32[16,32,256]{2,1,0:T(8,128)S(1)}, f32[16,32,256]{2,1,0:T(8,128)}, u32[]{:S(2)}) copy-start(f32[16,32,256]{2,1,0:T(8,128)} %cotangent.1) | copy-start | bytes 1572868
  1.7 0.7 %copy-start.3 = (f32[4,8,8]{2,1,0:T(8,128)S(1)}, f32[4,8,8]{2,1,0:T(8,128)}, u32[]{:S(2)}) copy-start(f32[4,8,8]{2,1,0:T(8,128)} %noise_k.1) | copy-start | bytes 3076
  2.4 0.8 %copy-start.5 = (f32[8,16,128]{2,1,0:T(8,128)S(1)}, f32[8,16,128]{2,1,0:T(8,128)}, u32[]{:S(2)}) copy-start(f32[8,16,128]{2,1,0:T(8,128)} %refs_3_.1) | copy-start | bytes 196612
  3.2 0.7 %copy-start.6 = (f32[4,8,64]{2,1,0:T(8,128)S(1)}, f32[4,8,64]{2,1,0:T(8,128)}, u32[]{:S(2)}) copy-start(f32[4,8,64]{2,1,0:T(8,128)} %refs_2_.1) | copy-start | bytes 24580
  4.0 0.7 %copy-start.7 = (f32[4,8,27]{2,1,0:T(8,128)S(1)}, f32[4,8,27]{2,1,0:T(8,128)}, u32[]{:S(2)}) copy-start(f32[4,8,27]{2,1,0:T(8,128)} %refs_4_.1) | copy-start | bytes 10372
  4.7 0.7 %copy-start.8 = (f32[2,4,32]{2,1,0:T(4,128)S(1)}, f32[2,4,32]{2,1,0:T(4,128)}, u32[]{:S(2)}) copy-start(f32[2,4,32]{2,1,0:T(4,128)} %refs_1_.1) | copy-start | bytes 3076
  5.4 0.7 %copy-start.9 = (f32[1,2,16]{2,1,0:T(2,128)S(1)}, f32[1,2,16]{2,1,0:T(2,128)}, u32[]{:S(2)}) copy-start(f32[1,2,16]{2,1,0:T(2,128)} %refs_0_.1) | copy-start | bytes 388
  6.0 27.7 %copy-start.1 = (f32[16,32,256]{2,1,0:T(8,128)S(1)}, f32[16,32,256]{2,1,0:T(8,128)}, u32[]{:S(2)}) copy-start(f32[16,32,256]{2,1,0:T(8,128)} %cotangent.1) | copy-start | bytes 1572868
  6.0 27.7 %copy-start.4 = (f32[4,8,8]{2,1,0:T(8,128)S(1)}, f32[4,8,8]{2,1,0:T(8,128)}, u32[]{:S(2)}) copy-start(f32[4,8,8]{2,1,0:T(8,128)} %noise_k.1) | copy-start | bytes 3076
  33.7 1.0 %copy-start.2 = (f32[16,32,256]{2,1,0:T(8,128)S(1)}, f32[16,32,256]{2,1,0:T(8,128)}, u32[]{:S(2)}) copy-start(f32[16,32,256]{2,1,0:T(8,128)} %noise.1) | copy-start | bytes 1572868
where the time goes:
time: 40 us; the launch traced here: 39.5 us
  Pallas kernels  32.4 us (81%)
  local copies, waits for them, and re-layouts  6.43 us (16%)
  between operations  0.68 us (2%)
    pallas_call x1, Pallas kernels, body(): pl.pallas_call(lambda *refs: main_kernel(plan, *refs), out_shape=[jax.Sha...  27.7 us
    unnamed x20, local copies, waits for them, and re-layouts  6.43 us
    pallas_call x1, Pallas kernels, body(): pl.pallas_call(finish_kernel, grid=(steps,), out_shape=[jax.ShapeDtypeStr...  4.76 us

commit v1 on v0

v1 whole, which is shorter than its diff:
```python
import jax
import jax.numpy as jnp
from jax import lax
from jax.experimental import pallas as pl
from jax.experimental.pallas import tpu as pltpu
from jax.sharding import PartitionSpec as P

LEVELS = 4
F32 = jnp.float32
BF16 = jnp.bfloat16
MESH = pl.DeviceIdType.MESH

NEAR = [(dx, dy) for dx in (-1, 0, 1) for dy in (-1, 0, 1) if (dx, dy) != (0, 0)]
FAR = [(dx, dy) for dx in (-2, 2) for dy in (-1, 0, 1)]
DIRS = NEAR + FAR


def up8(n):
    return -(-n // 8) * 8


class Plan:
    def __init__(self, shapes):
        self.block = shapes
        self.pairs = {}
        for level in range(1, LEVELS + 1):
            grow = 0 if level == LEVELS else 2
            self.pairs[level] = (shapes[level][0] // 2 + grow, shapes[level][1] // 2 + grow)
        self.rows = {level: up8(2 * ny) for level, (_, ny) in self.pairs.items()}
        self.ext = [
            (shapes[level][0] + 4, up8(shapes[level][1] + 4), 128) for level in range(LEVELS)
        ]
        self.pieces = {}
        self.offset = {}
        total = 0
        for dx, dy in DIRS:
            rows = 0
            pieces = []
            for level in range(LEVELS):
                if abs(dx) == 2 and level > 0:
                    continue
                bx, by = shapes[level][0], shapes[level][1]
                count_x = bx if dx == 0 else min(2, bx)
                count_y = by if dy == 0 else 2
                pieces.append((level, rows, count_x, count_y))
                rows += count_x * count_y
            self.pieces[dx, dy] = pieces
            self.offset[dx, dy] = (total, up8(rows))
            total += up8(rows)
        self.message_rows = total


def inner(step, size):
    if step == 0 or size == 1:
        return 2
    return 2 if step < 0 else size


def outer(step, size):
    if step == 0:
        return 2
    if size == 1:
        return 2 + step
    return 0 if step < 0 else size + 2


def lane_iota(shape):
    return lax.broadcasted_iota(jnp.int32, shape, len(shape) - 1)


def row_iota(shape):
    return lax.broadcasted_iota(jnp.int32, shape, len(shape) - 2)


def split(values):
    high = values.astype(BF16)
    return high, (values - high.astype(F32)).astype(BF16)


def select_dot(values, matrix):
    high, low = split(values)
    return jnp.dot(high, matrix, preferred_element_type=F32) + jnp.dot(
        low, matrix, preferred_element_type=F32
    )


def merge_matrix(size, width):
    row, col = row_iota((256, width)), lane_iota((256, width))
    parity = (row >= 128).astype(jnp.int32)
    at = row - 128 * parity
    return jnp.where((col == 2 * at + parity) & (at < size), 1.0, 0.0).astype(BF16)


def part_matrix(size, width):
    row, col = row_iota((width, 256)), lane_iota((width, 256))
    parity = (col >= 128).astype(jnp.int32)
    at = col - 128 * parity
    return jnp.where((row == 2 * at + parity) & (at < size), 1.0, 0.0).astype(BF16)


def parities():
    shape = (8, 128)
    return row_iota(shape) % 2 == 0, lane_iota(shape) % 2 == 0


def noise_patterns(read, store, transpose):
    even_row, even_lane = parities()
    for p in range(2):
        for other in range(2):
            for dq in range(2):
                for dr in range(2):
                    value = {}
                    for q in range(2):
                        for r in range(2):
                            here = 4 * p + 2 * q + r
                            there = 4 * other + 2 * (q ^ dq) + (r ^ dr)
                            value[q, r] = read(there, here) if transpose else read(here, there)
                    store(
                        p * 8 + other * 4 + dq * 2 + dr,
                        jnp.where(
                            even_row,
                            jnp.where(even_lane, value[0, 0], value[0, 1]),
                            jnp.where(even_lane, value[1, 0], value[1, 1]),
                        ),
                    )


def swaps(tile):
    even_row, even_lane = parities()

    def lanes(v):
        return jnp.where(even_lane, pltpu.roll(v, 127, 1), pltpu.roll(v, 1, 1))

    turned = jnp.where(even_row, pltpu.roll(tile, 7, 0), pltpu.roll(tile, 1, 0))
    return [tile, lanes(tile), turned, lanes(turned)]


def mix(first, second, weights):
    terms = swaps(first) + swaps(second)
    results = []
    for p in range(2):
        total = weights[p * 8] * terms[0]
        for at in range(1, 8):
            total = total + weights[p * 8 + at] * terms[at]
        results.append(total)
    return results


def shift_down(values, size):
    lane = lane_iota(values.shape)
    return jnp.where((lane > 0) & (lane < size), pltpu.roll(values, 1, 1), 0.0)


def shift_up(values, size):
    lane = lane_iota(values.shape)
    return jnp.where(lane < size - 1, pltpu.roll(values, 127, 1), 0.0)


def loop(count, step, unroll):
    if unroll >= count:
        for i in range(count):
            step(i)
        return

    def one(i, carry):
        step(i)
        return carry

    lax.fori_loop(0, count, one, 0, unroll=unroll)


UNROLL_MAIN = {1: 8, 2: 8, 3: 8, 4: 1}
UNROLL_SIDE = {1: 16, 2: 16, 3: 16, 4: 16}
UNROLL_MIX = {1: 16, 2: 16, 3: 16, 4: 1}


def main_kernel(
    plan,
    noise0, noise1, noise2, noise3, noise4, refine_hbm, noise_hbm, cotangent,
    density, grad0, grad1, grad2, grad3, grad4,
    own0, own1, own2, own3, refine_k, noise_k,
    ext0, ext1, ext2, ext3, part0, part1, part2, part3,
    field1, field2, field3, grads1, grads2, grads3,
    taps1, taps2, taps3, taps4,
    pattern, mixing, mixing_t, merges, parts, merge_last, part_last,
    cot, excite, spread, sums, turned,
    send_a, recv_a, send_b, recv_b,
    own_sem, table_sem, cot_sem, excite_sem,
    send_a_sem, recv_a_sem, send_b_sem, recv_b_sem,
):
    group, brick = lax.axis_index("group"), lax.axis_index("brick")
    groups, bricks = lax.axis_size("group"), lax.axis_size("brick")
    ext = [ext0, ext1, ext2, ext3]
    part = [part0, part1, part2, part3]
    field = [ext0, field1, field2, field3]
    grads = [part0, grads1, grads2, grads3]
    taps = [None, taps1, taps2, taps3, taps4]

    def neighbour(dx, dy):
        return (
            lax.rem(group + (dx + groups), groups),
            lax.rem(brick + (dy + bricks), bricks),
        )

    own = [own0, own1, own2, own3]
    own_copies = []
    for at, source in enumerate((noise0, noise1, noise2, noise3)):
        own_copies.append(pltpu.make_async_copy(source, own[at], own_sem.at[at]))
    table_copies = [
        pltpu.make_async_copy(refine_hbm, refine_k, table_sem.at[0]),
        pltpu.make_async_copy(noise_hbm, noise_k, table_sem.at[1]),
    ]
    cot_chunks = cot_sem.shape[0]
    chunk = cot.shape[0] // cot_chunks
    cot_copies = [
        pltpu.make_async_copy(
            cotangent.at[pl.ds(at * chunk, chunk)], cot.at[pl.ds(at * chunk, chunk)], cot_sem.at[at]
        )
        for at in range(cot_chunks)
    ]
    excite_copy = pltpu.make_async_copy(noise4, excite, excite_sem.at[0])
    for copy in own_copies + table_copies + cot_copies + [excite_copy]:
        copy.start()

    barrier = pltpu.get_barrier_semaphore()
    for dx, dy in DIRS:
        pl.semaphore_signal(barrier, inc=1, device_id=neighbour(dx, dy), device_id_type=MESH)

    for level in range(LEVELS):
        ext[level][...] = jnp.zeros(ext[level].shape, F32)
        if level:
            grads[level][...] = jnp.zeros(grads[level].shape, F32)
        part[level][...] = jnp.zeros(part[level].shape, F32)
    send_a[...] = jnp.zeros(send_a.shape, F32)
    send_b[...] = jnp.zeros(send_b.shape, F32)
    for level in range(1, LEVELS + 1):
        nx, _ = plan.pairs[level]
        rows = plan.rows[level]
        for t in range(3):
            for x in range(nx + 2):
                taps[level][t, x, 0:8, :] = jnp.zeros((8, 128), F32)
                taps[level][t, x, 8 + rows : 16 + rows, :] = jnp.zeros((8, 128), F32)
            for x in (0, nx + 1):
                taps[level][t, x, 8 : 8 + rows, :] = jnp.zeros((rows, 128), F32)
        size = plan.block[level][2] // 2
        if level < LEVELS:
            merges[level - 1] = merge_matrix(size, 128)
            parts[level - 1] = part_matrix(size, 128)
        else:
            merge_last[...] = merge_matrix(size, 256)
            part_last[...] = part_matrix(size, 256)
    for level in range(LEVELS):
        bx, by, size = plan.block[level]
        own_copies[level].wait()
        ext[level][2 : 2 + bx, 2 : 2 + by, 0:size] = own[level][...]

    def pack(source, target, start_of, sign):
        for dx, dy in DIRS:
            base, _ = plan.offset[dx, dy]
            for level, row, count_x, count_y in plan.pieces[dx, dy]:
                bx, by, _ = plan.block[level]
                x0, y0 = start_of(sign * dx, bx), start_of(sign * dy, by)
                for i in range(count_x):
                    target[pl.ds(base + row + i * count_y, count_y), :] = source[level][
                        x0 + i, y0 : y0 + count_y, :
                    ]

    def unpack(source, target, start_of, add):
        for dx, dy in DIRS:
            base, _ = plan.offset[dx, dy]
            for level, row, count_x, count_y in plan.pieces[dx, dy]:
                bx, by, _ = plan.block[level]
                x0, y0 = start_of(-dx, bx), start_of(-dy, by)
                for i in range(count_x):
                    value = source[pl.ds(base + row + i * count_y, count_y), :]
                    if add:
                        value = value + target[level][x0 + i, y0 : y0 + count_y, :]
                    target[level][x0 + i, y0 : y0 + count_y, :] = value

    def copies(source, target, send_sem, recv_sem):
        made = []
        for at, (dx, dy) in enumerate(DIRS):
            base, rows = plan.offset[dx, dy]
            made.append(
                pltpu.make_async_remote_copy(
                    src_ref=source.at[pl.ds(base, rows)],
                    dst_ref=target.at[pl.ds(base, rows)],
                    send_sem=send_sem.at[at],
                    recv_sem=recv_sem.at[at],
                    device_id=neighbour(dx, dy),
                    device_id_type=MESH,
                )
            )
        return made

    pack(ext, send_a, inner, 1)
    for copy in table_copies:
        copy.wait()

    even_row, _ = parities()

    def build(level, carry):
        for o in range(27):
            for p in range(2):
                for r in range(2):
                    pattern[level, o * 4 + p * 2 + r] = jnp.where(
                        even_row,
                        refine_k[level, 4 * p + r, o],
                        refine_k[level, 4 * p + 2 + r, o],
                    )

        def read(u, v):
            return noise_k[level, u, v]

        def store(at, value):
            mixing[level, at] = value

        def store_t(at, value):
            mixing_t[level, at] = value

        noise_patterns(read, store, False)
        noise_patterns(read, store_t, True)
        return carry

    lax.fori_loop(0, LEVELS, build, 0)

    def inside(level, x_at, shape, first_row, first_x):
        bx, by, _ = plan.block[level]
        y = row_iota(shape) + (brick * by - 2 + first_row)
        x = group * bx - 2 + first_x + x_at
        limit = jnp.where((x >= 0) & (x < groups * bx), bricks * by, 0)
        return (y >= 0) & (y < limit)

    def tile_rows(at):
        return pl.ds(8 * at, 8)

    def adjoint(level):
        nx, ny = plan.pairs[level]
        rows = plan.rows[level]
        size = plan.block[level][2] // 2
        tiles = rows // 8
        tap = taps[level]

        def store_parts(both, x0, count):
            for r in range(2):
                flat = both[:, 128 * r : 128 * (r + 1)]
                for w, moved in enumerate((shift_up(flat, size), flat, shift_down(flat, size))):
                    turned[w, r, x0 : x0 + count, 0:rows, :] = moved.reshape(count, rows, 128)

        if level == LEVELS:
            for at in range(cot_chunks):
                cot_copies[at].wait()
                flat = cot[at * chunk : (at + 1) * chunk].reshape(chunk * rows, 256)
                store_parts(select_dot(flat, part_last[...]), at * chunk, chunk)
        else:
            flat = grads[level][:, 0:rows, :].reshape(2 * nx * rows, 128)
            store_parts(select_dot(flat, parts[level - 1]), 0, 2 * nx)

        for s in (1, 0, 2):
            weights = [pattern[level - 1, s * 36 + at] for at in range(36)]

            def step(i):
                for tile in range(tiles):
                    here = tile_rows(tile)
                    there = pl.ds(8 + 8 * tile, 8)
                    values = [
                        turned[w, r, 2 * i + p, here, :]
                        for w in range(3)
                        for p in range(2)
                        for r in range(2)
                    ]
                    for t in range(3):
                        total = weights[12 * t] * values[0]
                        for at in range(1, 12):
                            total = total + weights[12 * t + at] * values[at]
                        if s != 1:
                            total = total + tap[t, i + s, there, :]
                        tap[t, i + s, there, :] = total

            loop(nx, step, UNROLL_MAIN[level])

        target = grads[level - 1]
        first = 1 if level == LEVELS else 0

        def combine(x):
            total = None
            for t in range(3):
                for q in range(2):
                    value = tap[t, x, pl.ds(8 - 2 * t + q, ny + 2, stride=2), :]
                    total = value if total is None else total + value
            keep = inside(level - 1, x, (ny + 2, 128), first, first)
            target[x + first, first : first + ny + 2, :] = jnp.where(keep, total, 0.0)

        loop(nx + 2, combine, UNROLL_SIDE[level])

    def mix_level(level, source, target, weights_of, masked):
        nx, _ = plan.pairs[level]
        weights = [weights_of[level - 1, at] for at in range(16)]
        halves = source.shape[2] // 128

        def step(i):
            for tile in range(plan.rows[level] // 8):
                for half in range(halves):
                    here, lanes = tile_rows(tile), pl.ds(128 * half, 128)
                    mixed = mix(
                        source[2 * i, here, lanes], source[2 * i + 1, here, lanes], weights
                    )
                    for p in range(2):
                        value = mixed[p]
                        if masked:
                            value = value + target[2 * i + p, here, lanes]
                            keep = inside(level, 2 * i + p, (8, 128), 8 * tile, 0)
                            value = jnp.where(keep, value, 0.0)
                        target[2 * i + p, here, lanes] = value

        loop(nx, step, UNROLL_MIX[level])

    adjoint(LEVELS)
    pl.semaphore_wait(barrier, len(DIRS))
    out_a = copies(send_a, recv_a, send_a_sem, recv_a_sem)
    for copy in out_a:
        copy.start()

    for level in range(LEVELS - 1, 0, -1):
        mix_level(level, grads[level], part[level], mixing_t, False)
        adjoint(level)

    pack(part, send_b, outer, 1)
    out_b = copies(send_b, recv_b, send_b_sem, recv_b_sem)
    for copy in out_b:
        copy.start()
    mix_level(LEVELS, cot, grad4, mixing_t, False)
    excite_copy.wait()
    mix_level(LEVELS, excite, density, mixing, False)

    for copy in out_a:
        copy.wait_recv()
    unpack(recv_a, ext, outer, False)
    for x in range(ext0.shape[0]):
        keep = inside(0, x, ext0.shape[1:], 0, 0)
        ext0[x] = jnp.where(keep, ext0[x], 0.0)

    def forward(level):
        nx, ny = plan.pairs[level]
        rows = plan.rows[level]
        size = plan.block[level][2] // 2
        first = 1 if level == LEVELS else 0
        source = field[level - 1]
        count = up8(ny + 2)

        def widen(x):
            for tile in range(count // 8):
                value = source[x + first, pl.ds(first + 8 * tile, 8), :]
                for w, moved in enumerate((shift_down(value, size), value, shift_up(value, size))):
                    for q in range(2):
                        spread[w, x, pl.ds(16 * tile + q, 8, stride=2), :] = moved

        loop(nx + 2, widen, UNROLL_SIDE[level])

        for s in range(3):
            weights = [pattern[level - 1, s * 36 + at] for at in range(36)]

            def step(i):
                for tile in range(rows // 8):
                    here = tile_rows(tile)
                    totals = [None] * 4
                    for tap in range(9):
                        value = spread[tap % 3, i + s, pl.ds(8 * tile + 2 * (tap // 3), 8), :]
                        for at in range(4):
                            term = weights[tap * 4 + at] * value
                            totals[at] = term if totals[at] is None else totals[at] + term
                    for at in range(4):
                        p, r = at // 2, at % 2
                        value = totals[at]
                        if s:
                            value = value + sums[r, 2 * i + p, here, :]
                        sums[r, 2 * i + p, here, :] = value

            loop(nx, step, UNROLL_MAIN[level])

        def merged(x0, count_x, matrix):
            both = jnp.concatenate(
                [sums[r, x0 : x0 + count_x, 0:rows, :].reshape(count_x * rows, 128) for r in range(2)],
                axis=1,
            )
            return select_dot(both, matrix).reshape(count_x, rows, -1)

        if level < LEVELS:
            field[level][:, 0:rows, :] = merged(0, 2 * nx, merges[level - 1])
            mix_level(level, ext[level], field[level], mixing, True)
        else:
            for at in range(cot_chunks):
                here = slice(at * chunk, (at + 1) * chunk)
                density[here] = density[here] + merged(at * chunk, chunk, merge_last[...])

    for level in range(1, LEVELS + 1):
        forward(level)

    for copy in out_b:
        copy.wait_recv()
    unpack(recv_b, part, inner, True)
    for level, target in enumerate((grad0, grad1, grad2, grad3)):
        bx, by, size = plan.block[level]
        target[...] = part[level][2 : 2 + bx, 2 : 2 + by, 0:size]
    for copy in out_a + out_b:
        copy.wait_send()


def finish_kernel(*refs):
    count = (len(refs) - 1) // 2
    copies = [
        pltpu.make_async_copy(refs[at], refs[count + at], refs[-1].at[at]) for at in range(count)
    ]
    for copy in copies:
        copy.start()
    for copy in copies:
        copy.wait()


def pin(array):
    return pltpu.with_memory_space_constraint(array, pltpu.HBM)


def body(
    noise_level0,
    noise_level1,
    noise_level2,
    noise_level3,
    noise_level4,
    refine_kernels,
    noise_kernels,
    cotangent,
):
    noises = (noise_level0, noise_level1, noise_level2, noise_level3, noise_level4)
    plan = Plan([noise.shape for noise in noises])
    nx, ny = plan.pairs[LEVELS]
    rows = plan.rows[LEVELS]
    hbm = pl.BlockSpec(memory_space=pltpu.HBM)
    vmem = pl.BlockSpec(memory_space=pltpu.VMEM)
    size_z = noise_level4.shape[2]

    def scratch(*shape, dtype=F32):
        return pltpu.VMEM(shape, dtype)

    def field_shape(level):
        grown = plan.ext[level]
        return (grown[0], grown[1] + 8, 128)

    count = len(DIRS)
    dma = pltpu.SemaphoreType.DMA
    results = [
        jax.ShapeDtypeStruct(array.shape, F32)
        for array in (noise_level4, *noises[:LEVELS], cotangent)
    ]
    blocks = pl.pallas_call(
        lambda *refs: main_kernel(plan, *refs),
        out_shape=results,
        in_specs=[hbm] * 8,
        out_specs=[vmem] * 6,
        scratch_shapes=[scratch(*noise.shape) for noise in noises[:LEVELS]]
        + [pltpu.SMEM(table.shape, F32) for table in (refine_kernels, noise_kernels)]
        + [scratch(*shape) for shape in plan.ext]
        + [scratch(*shape) for shape in plan.ext]
        + [scratch(*field_shape(level)) for level in (1, 2, 3)]
        + [scratch(*plan.ext[level]) for level in (1, 2, 3)]
        + [
            scratch(3, plan.pairs[level][0] + 2, plan.rows[level] + 16, 128)
            for level in (1, 2, 3, 4)
        ]
        + [
            scratch(LEVELS, 108, 8, 128),
            scratch(LEVELS, 16, 8, 128),
            scratch(LEVELS, 16, 8, 128),
            scratch(LEVELS - 1, 256, 128, dtype=BF16),
            scratch(LEVELS - 1, 128, 256, dtype=BF16),
            scratch(256, size_z, dtype=BF16),
            scratch(size_z, 256, dtype=BF16),
            scratch(*cotangent.shape),
            scratch(*noise_level4.shape),
            scratch(3, nx + 2, 2 * up8(ny + 2), 128),
            scratch(2, 2 * nx, rows, 128),
            scratch(3, 2, 2 * nx, rows, 128),
        ]
        + [scratch(plan.message_rows, 128)] * 4
        + [dma((LEVELS,)), dma((2,)), dma((4,)), dma((1,))]
        + [dma((count,))] * 4,
        compiler_params=pltpu.CompilerParams(
            collective_id=0, has_side_effects=True, vmem_limit_bytes=32 * 1024 * 1024
        ),
    )(*[pin(noise) for noise in noises], pin(refine_kernels), pin(noise_kernels), pin(cotangent))

    return pl.pallas_call(
        finish_kernel,
        out_shape=[pltpu.HBM(result.shape, F32) for result in results],
        in_specs=[vmem] * 6,
        out_specs=[hbm] * 6,
        scratch_shapes=[dma((6,))],
        compiler_params=pltpu.CompilerParams(vmem_limit_bytes=8 * 1024 * 1024),
    )(*blocks)


def solution(mesh):
    placed = P("group", "brick", None)
    return jax.shard_map(
        body,
        mesh=mesh,
        in_specs=(placed,) * 5 + (P(), P(), placed),
        out_specs=(placed,) * 6,
        check_vma=False,
    )
```

time: 40 us -> 23.9 us (0.60)
  Pallas kernels: 32.4 us -> 23.1 us
  local copies, waits for them, and re-layouts: 6.43 us -> 0 us
    pallas_call x2, Pallas kernels: 32.4 us -> 23.1 us  [the longest x1 22.1 us: body(): pl.pallas_call(lambda *refs: main_kernel(plan, *refs), out_shape=results,...]
    unnamed x20 -> x0, local copies, waits for them, and re-layouts: 6.43 us -> none
where the time goes in v1:
time: 23.9 us; the launch traced here: 23.8 us
  Pallas kernels  23.1 us (97%)
  between operations  0.64 us (3%)
    pallas_call x1, Pallas kernels, body(): pl.pallas_call(lambda *refs: main_kernel(plan, *refs), out_shape=results,...  22.1 us
    pallas_call x1, Pallas kernels, body(): pl.pallas_call(finish_kernel, out_shape=[pltpu.HBM(result.shape, F32) for...  1.06 us

profile of v1, /device:TPU:1, one launch (start us, length us, event | category | flops | bytes accessed | tf_op | source)
XLA Modules:
  0.0 23.8 jit_solution(332617673855497342)
XLA Ops:
  0.6 22.1 %shard_map.127 = (f32[16,32,256]{2,1,0:T(8,128)S(1)}, f32[1,2,16]{2,1,0:T(2,128)S(1)}, f32[2,4,32]{2,1,0:T(4,128)S(1)}, f32[4,8,64]{2,1,0:T(8,128)S(1)}, f32[8,1...) custom-call(f32[1,2,16]{2,1,0:T(2,128)} %refs_0_.1, f32[2,4,32]{2,1,0:T(4,128)} %refs_1_.1, f32[4,8,64]{2,1,0:T(8,128)} %refs_2_.1, ...), custom_call_target="tpu_custom_call" | custom-call | tf_op jit(solution)/shard_map/pallas_call | solution.py:555
  22.7 1.1 %shard_map.128 = (f32[16,32,256]{2,1,0:T(8,128)}, f32[1,2,16]{2,1,0:T(2,128)}, f32[2,4,32]{2,1,0:T(4,128)}, f32[4,8,64]{2,1,0:T(8,128)}, f32[8,16,128]{2,1,0:T(8,128)}, /*index=5*/f32[16,32,256]{2,1,0:T(8,128)}) custom-call(f32[16,32,256]{2,1,0:T(8,128)S(1)} %get-tuple-element.12.refs_0_, f32[1,2,16]{2,1,0:T(2,128)S(1)} %get-tuple-element.13.refs_1_, ...), custom_call_target="tpu_custom_call" | custom-call | tf_op jit(solution)/shard_map/pallas_call | solution.py:592

commit v2 on v1

--- a/solution.py
+++ b/solution.py
@@ -171,7 +171,8 @@
 
 UNROLL_MAIN = {1: 8, 2: 8, 3: 8, 4: 1}
 UNROLL_SIDE = {1: 16, 2: 16, 3: 16, 4: 16}
-UNROLL_MIX = {1: 16, 2: 16, 3: 16, 4: 1}
+UNROLL_MIX = {1: 16, 2: 16, 3: 16, 4: 2}
+LINE = 8
 
 
 def main_kernel(
@@ -222,9 +223,20 @@
     for copy in own_copies + table_copies + cot_copies + [excite_copy]:
         copy.start()
 
+    def exists(dx, dy):
+        x, y = group + dx, brick + dy
+        return (x >= 0) & (x < groups) & (y >= 0) & (y < bricks)
+
+    recv_a[...] = jnp.zeros(recv_a.shape, F32)
+    recv_b[...] = jnp.zeros(recv_b.shape, F32)
     barrier = pltpu.get_barrier_semaphore()
+    partners = 0
     for dx, dy in DIRS:
-        pl.semaphore_signal(barrier, inc=1, device_id=neighbour(dx, dy), device_id_type=MESH)
+        partners = partners + exists(dx, dy).astype(jnp.int32)
+
+        @pl.when(exists(dx, dy))
+        def _():
+            pl.semaphore_signal(barrier, inc=1, device_id=neighbour(dx, dy), device_id_type=MESH)
 
     for level in range(LEVELS):
         ext[level][...] = jnp.zeros(ext[level].shape, F32)
@@ -293,7 +305,28 @@
             )
         return made
 
+    def start_all(made):
+        for (dx, dy), copy in zip(DIRS, made):
+            pl.when(exists(dx, dy))(copy.start)
+
+    def wait_sent(made):
+        for (dx, dy), copy in zip(DIRS, made):
+            pl.when(exists(dx, dy))(copy.wait_send)
+
+    def wait_received(made):
+        for (dx, dy), copy in zip(DIRS, made):
+            pl.when(exists(-dx, -dy))(copy.wait_recv)
+
     pack(ext, send_a, inner, 1)
+    out_a = copies(send_a, recv_a, send_a_sem, recv_a_sem)
+    out_b = copies(send_b, recv_b, send_b_sem, recv_b_sem)
+    first_row = lax.rem(brick, LINE) == 0
+
+    @pl.when(jnp.logical_not(first_row))
+    def _():
+        pl.semaphore_wait(barrier, partners)
+        start_all(out_a)
+
     for copy in table_copies:
         copy.wait()
 
@@ -369,13 +402,13 @@
                         for p in range(2)
                         for r in range(2)
                     ]
+                    totals = [None if s == 1 else tap[t, i + s, there, :] for t in range(3)]
+                    for at in range(12):
+                        for t in range(3):
+                            term = weights[12 * t + at] * values[at]
+                            totals[t] = term if totals[t] is None else totals[t] + term
                     for t in range(3):
-                        total = weights[12 * t] * values[0]
-                        for at in range(1, 12):
-                            total = total + weights[12 * t + at] * values[at]
-                        if s != 1:
-                            total = total + tap[t, i + s, there, :]
-                        tap[t, i + s, there, :] = total
+                        tap[t, i + s, there, :] = totals[t]
 
             loop(nx, step, UNROLL_MAIN[level])
 
@@ -416,25 +449,27 @@
         loop(nx, step, UNROLL_MIX[level])
 
     adjoint(LEVELS)
-    pl.semaphore_wait(barrier, len(DIRS))
-    out_a = copies(send_a, recv_a, send_a_sem, recv_a_sem)
-    for copy in out_a:
-        copy.start()
-
     for level in range(LEVELS - 1, 0, -1):
         mix_level(level, grads[level], part[level], mixing_t, False)
         adjoint(level)
 
     pack(part, send_b, outer, 1)
-    out_b = copies(send_b, recv_b, send_b_sem, recv_b_sem)
-    for copy in out_b:
-        copy.start()
+
+    @pl.when(jnp.logical_not(first_row))
+    def _():
+        start_all(out_b)
+
     mix_level(LEVELS, cot, grad4, mixing_t, False)
     excite_copy.wait()
     mix_level(LEVELS, excite, density, mixing, False)
 
-    for copy in out_a:
-        copy.wait_recv()
+    @pl.when(first_row)
+    def _():
+        pl.semaphore_wait(barrier, partners)
+        start_all(out_a)
+        start_all(out_b)
+
+    wait_received(out_a)
     unpack(recv_a, ext, outer, False)
     for x in range(ext0.shape[0]):
         keep = inside(0, x, ext0.shape[1:], 0, 0)
@@ -496,14 +531,13 @@
     for level in range(1, LEVELS + 1):
         forward(level)
 
-    for copy in out_b:
-        copy.wait_recv()
+    wait_received(out_b)
     unpack(recv_b, part, inner, True)
     for level, target in enumerate((grad0, grad1, grad2, grad3)):
         bx, by, size = plan.block[level]
         target[...] = part[level][2 : 2 + bx, 2 : 2 + by, 0:size]
-    for copy in out_a + out_b:
-        copy.wait_send()
+    wait_sent(out_a)
+    wait_sent(out_b)
 
 
 def finish_kernel(*refs):

time: 23.9 us -> 19.4 us (0.81)
  the two profiles are of different devices: /device:TPU:1 before, /device:TPU:24 now
where the time goes in v2:
time: 19.4 us; the launch traced here: 19.3 us
  Pallas kernels  18.6 us (96%)
  between operations  0.64 us (3%)
    pallas_call x1, Pallas kernels, body(): pl.pallas_call(lambda *refs: main_kernel(plan, *refs), out_shape=results,...  17.6 us
    pallas_call x1, Pallas kernels, body(): pl.pallas_call(finish_kernel, out_shape=[pltpu.HBM(result.shape, F32) for...  1.06 us

profile of v2, /device:TPU:24, one launch (start us, length us, event | category | flops | bytes accessed | tf_op | source)
XLA Modules:
  0.0 19.3 jit_solution(4072113750129918477)
XLA Ops:
  0.6 17.6 %shard_map.127 = (f32[16,32,256]{2,1,0:T(8,128)S(1)}, f32[1,2,16]{2,1,0:T(2,128)S(1)}, f32[2,4,32]{2,1,0:T(4,128)S(1)}, f32[4,8,64]{2,1,0:T(8,128)S(1)}, f32[8,1...) custom-call(f32[1,2,16]{2,1,0:T(2,128)} %refs_0_.1, f32[2,4,32]{2,1,0:T(4,128)} %refs_1_.1, f32[4,8,64]{2,1,0:T(8,128)} %refs_2_.1, ...), custom_call_target="tpu_custom_call" | custom-call | tf_op jit(solution)/shard_map/pallas_call | solution.py:589
  18.2 1.1 %shard_map.128 = (f32[16,32,256]{2,1,0:T(8,128)}, f32[1,2,16]{2,1,0:T(2,128)}, f32[2,4,32]{2,1,0:T(4,128)}, f32[4,8,64]{2,1,0:T(8,128)}, f32[8,16,128]{2,1,0:T(8,128)}, /*index=5*/f32[16,32,256]{2,1,0:T(8,128)}) custom-call(f32[16,32,256]{2,1,0:T(8,128)S(1)} %get-tuple-element.12.refs_0_, f32[1,2,16]{2,1,0:T(2,128)S(1)} %get-tuple-element.13.refs_1_, ...), custom_call_target="tpu_custom_call" | custom-call | tf_op jit(solution)/shard_map/pallas_call | solution.py:626

commit v3 on v2

--- a/solution.py
+++ b/solution.py
@@ -12,7 +12,7 @@
 
 NEAR = [(dx, dy) for dx in (-1, 0, 1) for dy in (-1, 0, 1) if (dx, dy) != (0, 0)]
 FAR = [(dx, dy) for dx in (-2, 2) for dy in (-1, 0, 1)]
-DIRS = NEAR + FAR
+DIRS = sorted(NEAR + FAR, key=lambda step: (-step[1], abs(step[0])))
 
 
 def up8(n):
@@ -169,7 +169,7 @@
     lax.fori_loop(0, count, one, 0, unroll=unroll)
 
 
-UNROLL_MAIN = {1: 8, 2: 8, 3: 8, 4: 1}
+UNROLL_MAIN = {1: 8, 2: 8, 3: 8, 4: 4}
 UNROLL_SIDE = {1: 16, 2: 16, 3: 16, 4: 16}
 UNROLL_MIX = {1: 16, 2: 16, 3: 16, 4: 2}
 LINE = 8
@@ -183,7 +183,7 @@
     ext0, ext1, ext2, ext3, part0, part1, part2, part3,
     field1, field2, field3, grads1, grads2, grads3,
     taps1, taps2, taps3, taps4,
-    pattern, mixing, mixing_t, merges, parts, merge_last, part_last,
+    pattern, mixing, mixing_t, wide, merges, parts, merge_last, part_last,
     cot, excite, spread, sums, turned,
     send_a, recv_a, send_b, recv_b,
     own_sem, table_sem, cot_sem, excite_sem,
@@ -220,7 +220,7 @@
         for at in range(cot_chunks)
     ]
     excite_copy = pltpu.make_async_copy(noise4, excite, excite_sem.at[0])
-    for copy in own_copies + table_copies + cot_copies + [excite_copy]:
+    for copy in table_copies + cot_copies + own_copies + [excite_copy]:
         copy.start()
 
     def exists(dx, dy):
@@ -244,6 +244,66 @@
             grads[level][...] = jnp.zeros(grads[level].shape, F32)
         part[level][...] = jnp.zeros(part[level].shape, F32)
     send_a[...] = jnp.zeros(send_a.shape, F32)
+    def pack(source, target, start_of, sign, steps):
+        for dx, dy in steps:
+            base, _ = plan.offset[dx, dy]
+            for level, row, count_x, count_y in plan.pieces[dx, dy]:
+                bx, by, _ = plan.block[level]
+                x0, y0 = start_of(sign * dx, bx), start_of(sign * dy, by)
+                for i in range(count_x):
+                    target[pl.ds(base + row + i * count_y, count_y), :] = source[level][
+                        x0 + i, y0 : y0 + count_y, :
+                    ]
+
+    def unpack(source, target, start_of, add):
+        for dx, dy in DIRS:
+            base, _ = plan.offset[dx, dy]
+            for level, row, count_x, count_y in plan.pieces[dx, dy]:
+                bx, by, _ = plan.block[level]
+                x0, y0 = start_of(-dx, bx), start_of(-dy, by)
+                for i in range(count_x):
+                    value = source[pl.ds(base + row + i * count_y, count_y), :]
+                    if add:
+                        value = value + target[level][x0 + i, y0 : y0 + count_y, :]
+                    target[level][x0 + i, y0 : y0 + count_y, :] = value
+
+    def copies(source, target, send_sem, recv_sem):
+        made = []
+        for at, (dx, dy) in enumerate(DIRS):
+            base, rows = plan.offset[dx, dy]
+            made.append(
+                pltpu.make_async_remote_copy(
+                    src_ref=source.at[pl.ds(base, rows)],
+                    dst_ref=target.at[pl.ds(base, rows)],
+                    send_sem=send_sem.at[at],
+                    recv_sem=recv_sem.at[at],
+                    device_id=neighbour(dx, dy),
+                    device_id_type=MESH,
+                )
+            )
+        return made
+
+    def start(made, steps):
+        for (dx, dy), copy in zip(DIRS, made):
+            if (dx, dy) in steps:
+                pl.when(exists(dx, dy))(copy.start)
+
+    def wait_sent(made):
+        for (dx, dy), copy in zip(DIRS, made):
+            pl.when(exists(dx, dy))(copy.wait_send)
+
+    def wait_received(made):
+        for (dx, dy), copy in zip(DIRS, made):
+            pl.when(exists(-dx, -dy))(copy.wait_recv)
+
+    out_a = copies(send_a, recv_a, send_a_sem, recv_a_sem)
+    out_b = copies(send_b, recv_b, send_b_sem, recv_b_sem)
+    upward = [step for step in DIRS if step[1] > 0]
+    others = [step for step in DIRS if step[1] <= 0]
+    first_row = lax.rem(brick, LINE) == 0
+    last_row = lax.rem(brick, LINE) == LINE - 1
+    middle = jnp.logical_not(first_row | last_row)
+
     send_b[...] = jnp.zeros(send_b.shape, F32)
     for level in range(1, LEVELS + 1):
         nx, _ = plan.pairs[level]
@@ -261,101 +321,51 @@
         else:
             merge_last[...] = merge_matrix(size, 256)
             part_last[...] = part_matrix(size, 256)
+    def build_refine(level):
+        for p in range(2):
+            for r in range(2):
+                first, second = 4 * p + r, 4 * p + 2 + r
+                rows = jnp.where(
+                    row_iota((8, 27)) % 2 == 0,
+                    refine_k[level, first : first + 1, :],
+                    refine_k[level, second : second + 1, :],
+                )
+                for o in range(27):
+                    pattern[level, o * 4 + p * 2 + r] = jnp.broadcast_to(
+                        rows[:, o : o + 1], (8, 128)
+                    )
+
+    def build_mixing(level):
+        table = noise_k[level]
+        for v in range(8):
+            wide[level, v] = jnp.broadcast_to(table[:, v : v + 1], (8, 128))
+
+        def read(u, v):
+            return wide[level, v, u : u + 1, :]
+
+        def store(at, value):
+            mixing[level, at] = value
+
+        def store_t(at, value):
+            mixing_t[level, at] = value
+
+        noise_patterns(read, store, False)
+        noise_patterns(read, store_t, True)
+
+    for copy in table_copies:
+        copy.wait()
+    build_refine(LEVELS - 1)
     for level in range(LEVELS):
         bx, by, size = plan.block[level]
         own_copies[level].wait()
         ext[level][2 : 2 + bx, 2 : 2 + by, 0:size] = own[level][...]
 
-    def pack(source, target, start_of, sign):
-        for dx, dy in DIRS:
-            base, _ = plan.offset[dx, dy]
-            for level, row, count_x, count_y in plan.pieces[dx, dy]:
-                bx, by, _ = plan.block[level]
-                x0, y0 = start_of(sign * dx, bx), start_of(sign * dy, by)
-                for i in range(count_x):
-                    target[pl.ds(base + row + i * count_y, count_y), :] = source[level][
-                        x0 + i, y0 : y0 + count_y, :
-                    ]
-
-    def unpack(source, target, start_of, add):
-        for dx, dy in DIRS:
-            base, _ = plan.offset[dx, dy]
-            for level, row, count_x, count_y in plan.pieces[dx, dy]:
-                bx, by, _ = plan.block[level]
-                x0, y0 = start_of(-dx, bx), start_of(-dy, by)
-                for i in range(count_x):
-                    value = source[pl.ds(base + row + i * count_y, count_y), :]
-                    if add:
-                        value = value + target[level][x0 + i, y0 : y0 + count_y, :]
-                    target[level][x0 + i, y0 : y0 + count_y, :] = value
-
-    def copies(source, target, send_sem, recv_sem):
-        made = []
-        for at, (dx, dy) in enumerate(DIRS):
-            base, rows = plan.offset[dx, dy]
-            made.append(
-                pltpu.make_async_remote_copy(
-                    src_ref=source.at[pl.ds(base, rows)],
-                    dst_ref=target.at[pl.ds(base, rows)],
-                    send_sem=send_sem.at[at],
-                    recv_sem=recv_sem.at[at],
-                    device_id=neighbour(dx, dy),
-                    device_id_type=MESH,
-                )
-            )
-        return made
-
-    def start_all(made):
-        for (dx, dy), copy in zip(DIRS, made):
-            pl.when(exists(dx, dy))(copy.start)
-
-    def wait_sent(made):
-        for (dx, dy), copy in zip(DIRS, made):
-            pl.when(exists(dx, dy))(copy.wait_send)
-
-    def wait_received(made):
-        for (dx, dy), copy in zip(DIRS, made):
-            pl.when(exists(-dx, -dy))(copy.wait_recv)
-
-    pack(ext, send_a, inner, 1)
-    out_a = copies(send_a, recv_a, send_a_sem, recv_a_sem)
-    out_b = copies(send_b, recv_b, send_b_sem, recv_b_sem)
-    first_row = lax.rem(brick, LINE) == 0
-
-    @pl.when(jnp.logical_not(first_row))
+    pack(ext, send_a, inner, 1, DIRS)
+
+    @pl.when(last_row)
     def _():
         pl.semaphore_wait(barrier, partners)
-        start_all(out_a)
-
-    for copy in table_copies:
-        copy.wait()
-
-    even_row, _ = parities()
-
-    def build(level, carry):
-        for o in range(27):
-            for p in range(2):
-                for r in range(2):
-                    pattern[level, o * 4 + p * 2 + r] = jnp.where(
-                        even_row,
-                        refine_k[level, 4 * p + r, o],
-                        refine_k[level, 4 * p + 2 + r, o],
-                    )
-
-        def read(u, v):
-            return noise_k[level, u, v]
-
-        def store(at, value):
-            mixing[level, at] = value
-
-        def store_t(at, value):
-            mixing_t[level, at] = value
-
-        noise_patterns(read, store, False)
-        noise_patterns(read, store_t, True)
-        return carry
-
-    lax.fori_loop(0, LEVELS, build, 0)
+        start(out_a, upward)
 
     def inside(level, x_at, shape, first_row, first_x):
         bx, by, _ = plan.block[level]
@@ -449,25 +459,48 @@
         loop(nx, step, UNROLL_MIX[level])
 
     adjoint(LEVELS)
+
+    @pl.when(middle)
+    def _():
+        pl.semaphore_wait(barrier, partners)
+        start(out_a, DIRS)
+
     for level in range(LEVELS - 1, 0, -1):
+        build_mixing(level - 1)
+        build_refine(level - 1)
         mix_level(level, grads[level], part[level], mixing_t, False)
         adjoint(level)
 
-    pack(part, send_b, outer, 1)
-
-    @pl.when(jnp.logical_not(first_row))
+    pack(part, send_b, outer, 1, upward)
+
+    @pl.when(last_row)
     def _():
-        start_all(out_b)
-
+        start(out_b, upward)
+
+    pack(part, send_b, outer, 1, others)
+
+    @pl.when(first_row)
+    def _():
+        pl.semaphore_wait(barrier, partners)
+
+    @pl.when(middle)
+    def _():
+        start(out_b, DIRS)
+
+    @pl.when(jnp.logical_not(middle))
+    def _():
+        start(out_a, others)
+        start(out_b, others)
+
+    @pl.when(first_row)
+    def _():
+        start(out_a, upward)
+        start(out_b, upward)
+
+    build_mixing(LEVELS - 1)
     mix_level(LEVELS, cot, grad4, mixing_t, False)
     excite_copy.wait()
     mix_level(LEVELS, excite, density, mixing, False)
-
-    @pl.when(first_row)
-    def _():
-        pl.semaphore_wait(barrier, partners)
-        start_all(out_a)
-        start_all(out_b)
 
     wait_received(out_a)
     unpack(recv_a, ext, outer, False)
@@ -592,7 +625,7 @@
         in_specs=[hbm] * 8,
         out_specs=[vmem] * 6,
         scratch_shapes=[scratch(*noise.shape) for noise in noises[:LEVELS]]
-        + [pltpu.SMEM(table.shape, F32) for table in (refine_kernels, noise_kernels)]
+        + [scratch(*table.shape) for table in (refine_kernels, noise_kernels)]
         + [scratch(*shape) for shape in plan.ext]
         + [scratch(*shape) for shape in plan.ext]
         + [scratch(*field_shape(level)) for level in (1, 2, 3)]
@@ -605,6 +638,7 @@
             scratch(LEVELS, 108, 8, 128),
             scratch(LEVELS, 16, 8, 128),
             scratch(LEVELS, 16, 8, 128),
+            scratch(LEVELS, 8, 8, 128),
             scratch(LEVELS - 1, 256, 128, dtype=BF16),
             scratch(LEVELS - 1, 128, 256, dtype=BF16),
             scratch(256, size_z, dtype=BF16),

time: 19.4 us -> 18.4 us (0.948)
  Pallas kernels: 18.6 us -> 17.7 us
    pallas_call x1, Pallas kernels: 17.6 us -> 16.6 us  [body(): pl.pallas_call(lambda *refs: main_kernel(plan, *refs), out_shape=results,...]
where the time goes in v3:
time: 18.4 us; the launch traced here: 18.3 us
  Pallas kernels  17.7 us (96%)
  between operations  0.64 us (3%)
    pallas_call x1, Pallas kernels, body(): pl.pallas_call(lambda *refs: main_kernel(plan, *refs), out_shape=results,...  16.6 us
    pallas_call x1, Pallas kernels, body(): pl.pallas_call(finish_kernel, out_shape=[pltpu.HBM(result.shape, F32) for...  1.06 us

profile of v3, /device:TPU:24, one launch (start us, length us, event | category | flops | bytes accessed | tf_op | source)
XLA Modules:
  0.0 18.3 jit_solution(17343845738401714078)
XLA Ops:
  0.6 16.6 %shard_map.127 = (f32[16,32,256]{2,1,0:T(8,128)S(1)}, f32[1,2,16]{2,1,0:T(2,128)S(1)}, f32[2,4,32]{2,1,0:T(4,128)S(1)}, f32[4,8,64]{2,1,0:T(8,128)S(1)}, f32[8,1...) custom-call(f32[1,2,16]{2,1,0:T(2,128)} %refs_0_.1, f32[2,4,32]{2,1,0:T(4,128)} %refs_1_.1, f32[4,8,64]{2,1,0:T(8,128)} %refs_2_.1, ...), custom_call_target="tpu_custom_call" | custom-call | tf_op jit(solution)/shard_map/pallas_call | solution.py:622
  17.2 1.1 %shard_map.128 = (f32[16,32,256]{2,1,0:T(8,128)}, f32[1,2,16]{2,1,0:T(2,128)}, f32[2,4,32]{2,1,0:T(4,128)}, f32[4,8,64]{2,1,0:T(8,128)}, f32[8,16,128]{2,1,0:T(8,128)}, /*index=5*/f32[16,32,256]{2,1,0:T(8,128)}) custom-call(f32[16,32,256]{2,1,0:T(8,128)S(1)} %get-tuple-element.12.refs_0_, f32[1,2,16]{2,1,0:T(2,128)S(1)} %get-tuple-element.13.refs_1_, ...), custom_call_target="tpu_custom_call" | custom-call | tf_op jit(solution)/shard_map/pallas_call | solution.py:660

commit v4 on v3

--- a/solution.py
+++ b/solution.py
@@ -84,18 +84,22 @@
     )
 
 
-def merge_matrix(size, width):
-    row, col = row_iota((256, width)), lane_iota((256, width))
-    parity = (row >= 128).astype(jnp.int32)
-    at = row - 128 * parity
+def merge_matrix(size, width, half):
+    row, col = row_iota((2 * half, width)), lane_iota((2 * half, width))
+    parity = (row >= half).astype(jnp.int32)
+    at = row - half * parity
     return jnp.where((col == 2 * at + parity) & (at < size), 1.0, 0.0).astype(BF16)
 
 
-def part_matrix(size, width):
-    row, col = row_iota((width, 256)), lane_iota((width, 256))
-    parity = (col >= 128).astype(jnp.int32)
-    at = col - 128 * parity
-    return jnp.where((row == 2 * at + parity) & (at < size), 1.0, 0.0).astype(BF16)
+def part_matrix(size, width, half, fold):
+    row, col = row_iota((width, 2 * half)), lane_iota((width, 2 * half))
+    parity = (col >= half).astype(jnp.int32)
+    at = col - half * parity
+    fine = 2 * at + parity
+    found = row == fine
+    if fold:
+        found = found | (row == fine + half)
+    return jnp.where(found & (at < size), 1.0, 0.0).astype(BF16)
 
 
 def parities():
@@ -146,13 +150,13 @@
     return results
 
 
-def shift_down(values, size):
-    lane = lane_iota(values.shape)
+def shift_down(values, size, half):
+    lane = lane_iota(values.shape) % half
     return jnp.where((lane > 0) & (lane < size), pltpu.roll(values, 1, 1), 0.0)
 
 
-def shift_up(values, size):
-    lane = lane_iota(values.shape)
+def shift_up(values, size, half):
+    lane = lane_iota(values.shape) % half
     return jnp.where(lane < size - 1, pltpu.roll(values, 127, 1), 0.0)
 
 
@@ -173,6 +177,7 @@
 UNROLL_SIDE = {1: 16, 2: 16, 3: 16, 4: 16}
 UNROLL_MIX = {1: 16, 2: 16, 3: 16, 4: 2}
 LINE = 8
+HALF = 64
 
 
 def main_kernel(
@@ -255,8 +260,8 @@
                         x0 + i, y0 : y0 + count_y, :
                     ]
 
-    def unpack(source, target, start_of, add):
-        for dx, dy in DIRS:
+    def unpack(source, target, start_of, add, steps):
+        for dx, dy in steps:
             base, _ = plan.offset[dx, dy]
             for level, row, count_x, count_y in plan.pieces[dx, dy]:
                 bx, by, _ = plan.block[level]
@@ -292,9 +297,10 @@
         for (dx, dy), copy in zip(DIRS, made):
             pl.when(exists(dx, dy))(copy.wait_send)
 
-    def wait_received(made):
+    def wait_received(made, steps):
         for (dx, dy), copy in zip(DIRS, made):
-            pl.when(exists(-dx, -dy))(copy.wait_recv)
+            if (dx, dy) in steps:
+                pl.when(exists(-dx, -dy))(copy.wait_recv)
 
     out_a = copies(send_a, recv_a, send_a_sem, recv_a_sem)
     out_b = copies(send_b, recv_b, send_b_sem, recv_b_sem)
@@ -316,24 +322,29 @@
                 taps[level][t, x, 8 : 8 + rows, :] = jnp.zeros((rows, 128), F32)
         size = plan.block[level][2] // 2
         if level < LEVELS:
-            merges[level - 1] = merge_matrix(size, 128)
-            parts[level - 1] = part_matrix(size, 128)
+            merges[level - 1] = merge_matrix(size, 128, HALF)
+            parts[level - 1] = part_matrix(size, 128, HALF, level < LEVELS - 1)
         else:
-            merge_last[...] = merge_matrix(size, 256)
-            part_last[...] = part_matrix(size, 256)
+            merge_last[...] = merge_matrix(size, 256, 128)
+            part_last[...] = part_matrix(size, 256, 128, False)
     def build_refine(level):
+        low = lane_iota((8, 128)) < HALF
         for p in range(2):
-            for r in range(2):
-                first, second = 4 * p + r, 4 * p + 2 + r
-                rows = jnp.where(
+            rows = [
+                jnp.where(
                     row_iota((8, 27)) % 2 == 0,
-                    refine_k[level, first : first + 1, :],
-                    refine_k[level, second : second + 1, :],
+                    refine_k[level, 4 * p + r : 4 * p + r + 1, :],
+                    refine_k[level, 4 * p + 2 + r : 4 * p + 3 + r, :],
                 )
-                for o in range(27):
-                    pattern[level, o * 4 + p * 2 + r] = jnp.broadcast_to(
-                        rows[:, o : o + 1], (8, 128)
-                    )
+                for r in range(2)
+            ]
+            for o in range(27):
+                tiles = [jnp.broadcast_to(rows[r][:, o : o + 1], (8, 128)) for r in range(2)]
+                if level == LEVELS - 1:
+                    for r in range(2):
+                        pattern[level, o * 4 + p * 2 + r] = tiles[r]
+                else:
+                    pattern[level, o * 2 + p] = jnp.where(low, tiles[0], tiles[1])
 
     def build_mixing(level):
         table = noise_k[level]
@@ -379,15 +390,18 @@
 
     def adjoint(level):
         nx, ny = plan.pairs[level]
+        halves, half = (2, 128) if level == LEVELS else (1, HALF)
         rows = plan.rows[level]
         size = plan.block[level][2] // 2
         tiles = rows // 8
         tap = taps[level]
 
         def store_parts(both, x0, count):
-            for r in range(2):
+            for r in range(halves):
                 flat = both[:, 128 * r : 128 * (r + 1)]
-                for w, moved in enumerate((shift_up(flat, size), flat, shift_down(flat, size))):
+                for w, moved in enumerate(
+                    (shift_up(flat, size, half), flat, shift_down(flat, size, half))
+                ):
                     turned[w, r, x0 : x0 + count, 0:rows, :] = moved.reshape(count, rows, 128)
 
         if level == LEVELS:
@@ -400,7 +414,7 @@
             store_parts(select_dot(flat, parts[level - 1]), 0, 2 * nx)
 
         for s in (1, 0, 2):
-            weights = [pattern[level - 1, s * 36 + at] for at in range(36)]
+            weights = [pattern[level - 1, s * 18 * halves + at] for at in range(18 * halves)]
 
             def step(i):
                 for tile in range(tiles):
@@ -410,12 +424,12 @@
                         turned[w, r, 2 * i + p, here, :]
                         for w in range(3)
                         for p in range(2)
-                        for r in range(2)
+                        for r in range(halves)
                     ]
                     totals = [None if s == 1 else tap[t, i + s, there, :] for t in range(3)]
-                    for at in range(12):
+                    for at in range(6 * halves):
                         for t in range(3):
-                            term = weights[12 * t + at] * values[at]
+                            term = weights[6 * halves * t + at] * values[at]
                             totals[t] = term if totals[t] is None else totals[t] + term
                     for t in range(3):
                         tap[t, i + s, there, :] = totals[t]
@@ -436,13 +450,13 @@
 
         loop(nx + 2, combine, UNROLL_SIDE[level])
 
-    def mix_level(level, source, target, weights_of, masked):
+    def mix_level(level, source, target, weights_of, masked, tiles=None):
         nx, _ = plan.pairs[level]
         weights = [weights_of[level - 1, at] for at in range(16)]
         halves = source.shape[2] // 128
 
         def step(i):
-            for tile in range(plan.rows[level] // 8):
+            for tile in range(plan.rows[level] // 8) if tiles is None else tiles:
                 for half in range(halves):
                     here, lanes = tile_rows(tile), pl.ds(128 * half, 128)
                     mixed = mix(
@@ -465,10 +479,14 @@
         pl.semaphore_wait(barrier, partners)
         start(out_a, DIRS)
 
+    def top_tiles(level):
+        by = plan.block[level][1]
+        return range((by + 2) // 8, (by + 3) // 8 + 1)
+
     for level in range(LEVELS - 1, 0, -1):
         build_mixing(level - 1)
         build_refine(level - 1)
-        mix_level(level, grads[level], part[level], mixing_t, False)
+        mix_level(level, grads[level], part[level], mixing_t, False, top_tiles(level))
         adjoint(level)
 
     pack(part, send_b, outer, 1, upward)
@@ -477,6 +495,11 @@
     def _():
         start(out_b, upward)
 
+    for level in range(LEVELS - 1, 0, -1):
+        done = top_tiles(level)
+        rest = [tile for tile in range(plan.rows[level] // 8) if tile not in done]
+        if rest:
+            mix_level(level, grads[level], part[level], mixing_t, False, rest)
     pack(part, send_b, outer, 1, others)
 
     @pl.when(first_row)
@@ -502,8 +525,9 @@
     excite_copy.wait()
     mix_level(LEVELS, excite, density, mixing, False)
 
-    wait_received(out_a)
-    unpack(recv_a, ext, outer, False)
+    for steps in (others, upward):
+        wait_received(out_a, steps)
+        unpack(recv_a, ext, outer, False, steps)
     for x in range(ext0.shape[0]):
         keep = inside(0, x, ext0.shape[1:], 0, 0)
         ext0[x] = jnp.where(keep, ext0[x], 0.0)
@@ -513,32 +537,37 @@
         rows = plan.rows[level]
         size = plan.block[level][2] // 2
         first = 1 if level == LEVELS else 0
+        halves, half = (2, 128) if level == LEVELS else (1, HALF)
         source = field[level - 1]
         count = up8(ny + 2)
 
         def widen(x):
             for tile in range(count // 8):
                 value = source[x + first, pl.ds(first + 8 * tile, 8), :]
-                for w, moved in enumerate((shift_down(value, size), value, shift_up(value, size))):
+                if level < LEVELS:
+                    value = value + pltpu.roll(value, HALF, 1)
+                for w, moved in enumerate(
+                    (shift_down(value, size, half), value, shift_up(value, size, half))
+                ):
                     for q in range(2):
                         spread[w, x, pl.ds(16 * tile + q, 8, stride=2), :] = moved
 
         loop(nx + 2, widen, UNROLL_SIDE[level])
 
         for s in range(3):
-            weights = [pattern[level - 1, s * 36 + at] for at in range(36)]
+            weights = [pattern[level - 1, s * 18 * halves + at] for at in range(18 * halves)]
 
             def step(i):
                 for tile in range(rows // 8):
                     here = tile_rows(tile)
-                    totals = [None] * 4
+                    totals = [None] * (2 * halves)
                     for tap in range(9):
                         value = spread[tap % 3, i + s, pl.ds(8 * tile + 2 * (tap // 3), 8), :]
-                        for at in range(4):
-                            term = weights[tap * 4 + at] * value
+                        for at in range(2 * halves):
+                            term = weights[tap * 2 * halves + at] * value
                             totals[at] = term if totals[at] is None else totals[at] + term
-                    for at in range(4):
-                        p, r = at // 2, at % 2
+                    for at in range(2 * halves):
+                        p, r = at // halves, at % halves
                         value = totals[at]
                         if s:
                             value = value + sums[r, 2 * i + p, here, :]
@@ -548,7 +577,10 @@
 
         def merged(x0, count_x, matrix):
             both = jnp.concatenate(
-                [sums[r, x0 : x0 + count_x, 0:rows, :].reshape(count_x * rows, 128) for r in range(2)],
+                [
+                    sums[r, x0 : x0 + count_x, 0:rows, :].reshape(count_x * rows, 128)
+                    for r in range(halves)
+                ],
                 axis=1,
             )
             return select_dot(both, matrix).reshape(count_x, rows, -1)
@@ -564,11 +596,15 @@
     for level in range(1, LEVELS + 1):
         forward(level)
 
-    wait_received(out_b)
-    unpack(recv_b, part, inner, True)
+    for steps in (others, upward):
+        wait_received(out_b, steps)
+        unpack(recv_b, part, inner, True, steps)
     for level, target in enumerate((grad0, grad1, grad2, grad3)):
         bx, by, size = plan.block[level]
-        target[...] = part[level][2 : 2 + bx, 2 : 2 + by, 0:size]
+        total = part[level][2 : 2 + bx, 2 : 2 + by, 0:size]
+        if level < LEVELS - 1:
+            total = total + part[level][2 : 2 + bx, 2 : 2 + by, HALF : HALF + size]
+        target[...] = total
     wait_sent(out_a)
     wait_sent(out_b)
 
@@ -639,8 +675,8 @@
             scratch(LEVELS, 16, 8, 128),
             scratch(LEVELS, 16, 8, 128),
             scratch(LEVELS, 8, 8, 128),
-            scratch(LEVELS - 1, 256, 128, dtype=BF16),
-            scratch(LEVELS - 1, 128, 256, dtype=BF16),
+            scratch(LEVELS - 1, 128, 128, dtype=BF16),
+            scratch(LEVELS - 1, 128, 128, dtype=BF16),
             scratch(256, size_z, dtype=BF16),
             scratch(size_z, 256, dtype=BF16),
             scratch(*cotangent.shape),

time: 18.4 us -> 17.5 us (0.951)
  Pallas kernels: 17.7 us -> 16.8 us
    pallas_call x1, Pallas kernels: 16.6 us -> 15.7 us  [body(): pl.pallas_call(lambda *refs: main_kernel(plan, *refs), out_shape=results,...]
where the time goes in v4:
time: 17.5 us; the launch traced here: 17.4 us
  Pallas kernels  16.8 us (96%)
  between operations  0.64 us (4%)
    pallas_call x1, Pallas kernels, body(): pl.pallas_call(lambda *refs: main_kernel(plan, *refs), out_shape=results,...  15.7 us
    pallas_call x1, Pallas kernels, body(): pl.pallas_call(finish_kernel, out_shape=[pltpu.HBM(result.shape, F32) for...  1.06 us

profile of v4, /device:TPU:24, one launch (start us, length us, event | category | flops | bytes accessed | tf_op | source)
XLA Modules:
  0.0 17.4 jit_solution(8641281244073895851)
XLA Ops:
  0.6 15.7 %shard_map.127 = (f32[16,32,256]{2,1,0:T(8,128)S(1)}, f32[1,2,16]{2,1,0:T(2,128)S(1)}, f32[2,4,32]{2,1,0:T(4,128)S(1)}, f32[4,8,64]{2,1,0:T(8,128)S(1)}, f32[8,1...) custom-call(f32[1,2,16]{2,1,0:T(2,128)} %refs_0_.1, f32[2,4,32]{2,1,0:T(4,128)} %refs_1_.1, f32[4,8,64]{2,1,0:T(8,128)} %refs_2_.1, ...), custom_call_target="tpu_custom_call" | custom-call | tf_op jit(solution)/shard_map/pallas_call | solution.py:658
  16.4 1.1 %shard_map.128 = (f32[16,32,256]{2,1,0:T(8,128)}, f32[1,2,16]{2,1,0:T(2,128)}, f32[2,4,32]{2,1,0:T(4,128)}, f32[4,8,64]{2,1,0:T(8,128)}, f32[8,16,128]{2,1,0:T(8,128)}, /*index=5*/f32[16,32,256]{2,1,0:T(8,128)}) custom-call(f32[16,32,256]{2,1,0:T(8,128)S(1)} %get-tuple-element.12.refs_0_, f32[1,2,16]{2,1,0:T(2,128)S(1)} %get-tuple-element.13.refs_1_, ...), custom_call_target="tpu_custom_call" | custom-call | tf_op jit(solution)/shard_map/pallas_call | solution.py:696

commit v5 on v4

--- a/solution.py
+++ b/solution.py
@@ -173,9 +173,9 @@
     lax.fori_loop(0, count, one, 0, unroll=unroll)
 
 
-UNROLL_MAIN = {1: 8, 2: 8, 3: 8, 4: 4}
+UNROLL_MAIN = {1: 8, 2: 8, 3: 8, 4: 8}
 UNROLL_SIDE = {1: 16, 2: 16, 3: 16, 4: 16}
-UNROLL_MIX = {1: 16, 2: 16, 3: 16, 4: 2}
+UNROLL_MIX = {1: 16, 2: 16, 3: 16, 4: 4}
 LINE = 8
 HALF = 64
 
@@ -225,7 +225,7 @@
         for at in range(cot_chunks)
     ]
     excite_copy = pltpu.make_async_copy(noise4, excite, excite_sem.at[0])
-    for copy in table_copies + cot_copies + own_copies + [excite_copy]:
+    for copy in cot_copies + table_copies + own_copies + [excite_copy]:
         copy.start()
 
     def exists(dx, dy):
@@ -596,7 +596,10 @@
     for level in range(1, LEVELS + 1):
         forward(level)
 
+    wait_sent(out_a)
     for steps in (others, upward):
+        if steps is upward:
+            wait_sent(out_b)
         wait_received(out_b, steps)
         unpack(recv_b, part, inner, True, steps)
     for level, target in enumerate((grad0, grad1, grad2, grad3)):
@@ -605,8 +608,6 @@
         if level < LEVELS - 1:
             total = total + part[level][2 : 2 + bx, 2 : 2 + by, HALF : HALF + size]
         target[...] = total
-    wait_sent(out_a)
-    wait_sent(out_b)
 
 
 def finish_kernel(*refs):
@@ -686,7 +687,7 @@
             scratch(3, 2, 2 * nx, rows, 128),
         ]
         + [scratch(plan.message_rows, 128)] * 4
-        + [dma((LEVELS,)), dma((2,)), dma((4,)), dma((1,))]
+        + [dma((LEVELS,)), dma((2,)), dma((1,)), dma((1,))]
         + [dma((count,))] * 4,
         compiler_params=pltpu.CompilerParams(
             collective_id=0, has_side_effects=True, vmem_limit_bytes=32 * 1024 * 1024

time: 17.5 us -> 16.7 us (0.954)
  Pallas kernels: 16.8 us -> 15.9 us
    pallas_call x1, Pallas kernels: 15.7 us -> 14.9 us  [body(): pl.pallas_call(lambda *refs: main_kernel(plan, *refs), out_shape=results,...]
where the time goes in v5:
time: 16.7 us; the launch traced here: 16.6 us
  Pallas kernels  15.9 us (95%)
  between operations  0.64 us (4%)
    pallas_call x1, Pallas kernels, body(): pl.pallas_call(lambda *refs: main_kernel(plan, *refs), out_shape=results,...  14.9 us
    pallas_call x1, Pallas kernels, body(): pl.pallas_call(finish_kernel, out_shape=[pltpu.HBM(result.shape, F32) for...  1.06 us

profile of v5, /device:TPU:24, one launch (start us, length us, event | category | flops | bytes accessed | tf_op | source)
XLA Modules:
  0.0 16.6 jit_solution(9180307267350531587)
XLA Ops:
  0.6 14.9 %shard_map.127 = (f32[16,32,256]{2,1,0:T(8,128)S(1)}, f32[1,2,16]{2,1,0:T(2,128)S(1)}, f32[2,4,32]{2,1,0:T(4,128)S(1)}, f32[4,8,64]{2,1,0:T(8,128)S(1)}, f32[8,1...) custom-call(f32[1,2,16]{2,1,0:T(2,128)} %refs_0_.1, f32[2,4,32]{2,1,0:T(4,128)} %refs_1_.1, f32[4,8,64]{2,1,0:T(8,128)} %refs_2_.1, ...), custom_call_target="tpu_custom_call" | custom-call | tf_op jit(solution)/shard_map/pallas_call | solution.py:659
  15.5 1.1 %shard_map.128 = (f32[16,32,256]{2,1,0:T(8,128)}, f32[1,2,16]{2,1,0:T(2,128)}, f32[2,4,32]{2,1,0:T(4,128)}, f32[4,8,64]{2,1,0:T(8,128)}, f32[8,16,128]{2,1,0:T(8,128)}, /*index=5*/f32[16,32,256]{2,1,0:T(8,128)}) custom-call(f32[16,32,256]{2,1,0:T(8,128)S(1)} %get-tuple-element.12.refs_0_, f32[1,2,16]{2,1,0:T(2,128)S(1)} %get-tuple-element.13.refs_1_, ...), custom_call_target="tpu_custom_call" | custom-call | tf_op jit(solution)/shard_map/pallas_call | solution.py:697

commit v6 on v5

--- a/solution.py
+++ b/solution.py
@@ -346,22 +346,19 @@
                 else:
                     pattern[level, o * 2 + p] = jnp.where(low, tiles[0], tiles[1])
 
-    def build_mixing(level):
+    def spread_mixing(level):
         table = noise_k[level]
         for v in range(8):
             wide[level, v] = jnp.broadcast_to(table[:, v : v + 1], (8, 128))
 
+    def build_mixing(level, target, transpose):
         def read(u, v):
             return wide[level, v, u : u + 1, :]
 
         def store(at, value):
-            mixing[level, at] = value
-
-        def store_t(at, value):
-            mixing_t[level, at] = value
-
-        noise_patterns(read, store, False)
-        noise_patterns(read, store_t, True)
+            target[level, at] = value
+
+        noise_patterns(read, store, transpose)
 
     for copy in table_copies:
         copy.wait()
@@ -484,7 +481,8 @@
         return range((by + 2) // 8, (by + 3) // 8 + 1)
 
     for level in range(LEVELS - 1, 0, -1):
-        build_mixing(level - 1)
+        spread_mixing(level - 1)
+        build_mixing(level - 1, mixing_t, True)
         build_refine(level - 1)
         mix_level(level, grads[level], part[level], mixing_t, False, top_tiles(level))
         adjoint(level)
@@ -520,7 +518,10 @@
         start(out_a, upward)
         start(out_b, upward)
 
-    build_mixing(LEVELS - 1)
+    spread_mixing(LEVELS - 1)
+    build_mixing(LEVELS - 1, mixing_t, True)
+    for level in range(LEVELS):
+        build_mixing(level, mixing, False)
     mix_level(LEVELS, cot, grad4, mixing_t, False)
     excite_copy.wait()
     mix_level(LEVELS, excite, density, mixing, False)
@@ -682,7 +683,7 @@
             scratch(size_z, 256, dtype=BF16),
             scratch(*cotangent.shape),
             scratch(*noise_level4.shape),
-            scratch(3, nx + 2, 2 * up8(ny + 2), 128),
+            scratch(3, nx + 2, 2 * up8(ny + 2) + 8, 128),
             scratch(2, 2 * nx, rows, 128),
             scratch(3, 2, 2 * nx, rows, 128),
         ]

time: 16.7 us -> 16.7 us (level)
  no operation moved by 1% of the time
where the time goes in v6:
time: 16.7 us; the launch traced here: 16.5 us
  Pallas kernels  15.9 us (95%)
  between operations  0.64 us (4%)
    pallas_call x1, Pallas kernels, body(): pl.pallas_call(lambda *refs: main_kernel(plan, *refs), out_shape=results,...  14.8 us
    pallas_call x1, Pallas kernels, body(): pl.pallas_call(finish_kernel, out_shape=[pltpu.HBM(result.shape, F32) for...  1.06 us

profile of v6, /device:TPU:24, one launch (start us, length us, event | category | flops | bytes accessed | tf_op | source)
XLA Modules:
  0.0 16.5 jit_solution(1581164179406312060)
XLA Ops:
  0.6 14.8 %shard_map.127 = (f32[16,32,256]{2,1,0:T(8,128)S(1)}, f32[1,2,16]{2,1,0:T(2,128)S(1)}, f32[2,4,32]{2,1,0:T(4,128)S(1)}, f32[4,8,64]{2,1,0:T(8,128)S(1)}, f32[8,1...) custom-call(f32[1,2,16]{2,1,0:T(2,128)} %refs_0_.1, f32[2,4,32]{2,1,0:T(4,128)} %refs_1_.1, f32[4,8,64]{2,1,0:T(8,128)} %refs_2_.1, ...), custom_call_target="tpu_custom_call" | custom-call | tf_op jit(solution)/shard_map/pallas_call | solution.py:660
  15.5 1.1 %shard_map.128 = (f32[16,32,256]{2,1,0:T(8,128)}, f32[1,2,16]{2,1,0:T(2,128)}, f32[2,4,32]{2,1,0:T(4,128)}, f32[4,8,64]{2,1,0:T(8,128)}, f32[8,16,128]{2,1,0:T(8,128)}, /*index=5*/f32[16,32,256]{2,1,0:T(8,128)}) custom-call(f32[16,32,256]{2,1,0:T(8,128)S(1)} %get-tuple-element.12.refs_0_, f32[1,2,16]{2,1,0:T(2,128)S(1)} %get-tuple-element.13.refs_1_, ...), custom_call_target="tpu_custom_call" | custom-call | tf_op jit(solution)/shard_map/pallas_call | solution.py:698
